TPU v7x, 512 devices: a whole 4x4x16 slice. The times are simulated.
512 devices in a mesh: prow: 32 (over y_lo, z), pcol: 16 (over y_hi, x, core).
Axes of the slice: x: 4, y: 4 (y_hi: 2, y_lo: 2; y = y_hi * 2 + y_lo), z: 16, core: 2. Of those that a mesh axis runs over, the one named last changes fastest.
Arguments:
- matrix: float32 [1, 8192, 2, 4096], P(None, 'prow', None, 'pcol'), may hold values from -6 to 6
- reflectors: float32 [1, 8192, 256], P(None, 'prow'), may hold values from -0.0625 to 0.0625
Outputs:
- updated: float32 [1, 8192, 2, 4096], P(None, 'prow', None, 'pcol')
All inputs are finite; a program needn't handle non-finite values.
Results may differ from a plain program's by a relative error of at most 0.0003.
Values sent between devices are 32-bit elements; how exact they have to be, the bound alone decides.
A program may use at most 64 MiB of HBM per device.

v0:
```python
import jax
import jax.numpy as jnp
from jax import lax
from jax.sharding import PartitionSpec as P

precise = lax.Precision.HIGHEST


def spread(shard, axis, root):
    mine = lax.axis_index(axis) == root
    return lax.psum(jnp.where(mine, shard, jnp.zeros_like(shard)), axis)


def invert_factor(gram_total):
    order = gram_total.shape[0]
    scale = 0.5 * jnp.diagonal(gram_total)
    nilpotent = jnp.triu(gram_total, 1) / scale[:, None]
    eye_matrix = jnp.eye(order, dtype=gram_total.dtype)
    power = -nilpotent
    result = eye_matrix + power
    exponent = 1
    while exponent < order:
        power = jnp.dot(power, power, precision=precise)
        result = jnp.dot(result, eye_matrix + power, precision=precise)
        exponent = exponent * 2
    return result / scale[None, :]


def mirror_rows(rows_part):
    pcol_count = lax.axis_size("pcol")
    col_index = lax.axis_index("pcol")
    tile_count, tile_rows, tile_cols = rows_part.shape
    halves = []
    for half_index in range(2):
        halves.append(spread(rows_part, "prow", col_index + half_index * pcol_count))
    received = jnp.stack(halves, axis=1)
    return received.reshape(2 * tile_count, tile_rows, tile_cols)


def column_to_rows(column_part):
    pcol_count = lax.axis_size("pcol")
    row_index = lax.axis_index("prow")
    tile_count, tile_rows, tile_cols = column_part.shape
    paired_tiles = column_part.reshape(tile_count // 2, 2, tile_rows, tile_cols)
    chosen = jnp.where(row_index // pcol_count == 0, paired_tiles[:, 0], paired_tiles[:, 1])
    return spread(chosen, "pcol", row_index % pcol_count)


def body(matrix, reflectors):
    prow_count = lax.axis_size("prow")
    pcol_count = lax.axis_size("pcol")
    row_index = lax.axis_index("prow")
    col_index = lax.axis_index("pcol")
    row_tiles, tile_rows, col_tiles, tile_cols = matrix.shape
    row_ids = jnp.arange(row_tiles, dtype=jnp.int32) * prow_count + row_index
    col_ids = jnp.arange(col_tiles, dtype=jnp.int32) * pcol_count + col_index
    strict = (row_ids[:, None] > col_ids[None, :])[:, None, :, None]
    on_diag = (row_ids[:, None] == col_ids[None, :])[:, None, :, None]
    lower_part = jnp.where(strict, matrix, jnp.where(on_diag, 0.5 * matrix, 0.0))
    within = jnp.arange(tile_rows, dtype=jnp.int32)[:, None]
    across = jnp.arange(reflectors.shape[2], dtype=jnp.int32)[None, :]
    unit_block = jnp.where(within > across, reflectors, jnp.where(within == across, 1.0, 0.0))
    ids_rows = row_ids[:, None, None]
    vec_rows = jnp.where(ids_rows == 0, 0.0, jnp.where(ids_rows == 1, unit_block, reflectors))
    vec_cols = mirror_rows(vec_rows)
    part_rows = jnp.einsum("racu,cub->rab", lower_part, vec_cols, precision=precise)
    part_cols = jnp.einsum("racu,rab->cub", lower_part, vec_rows, precision=precise)
    sums_rows = lax.psum(part_rows, "pcol")
    sums_cols = lax.psum(part_cols, "prow")
    image_cols = sums_cols + mirror_rows(sums_rows)
    gram_part = jnp.einsum("cub,cud->bd", vec_cols, vec_cols, precision=precise)
    cross_part = jnp.einsum("cub,cud->bd", vec_cols, image_cols, precision=precise)
    gram_total, cross_total = lax.psum((gram_part, cross_part), "pcol")
    coefficient = invert_factor(gram_total)
    middle = jnp.dot(
        jnp.dot(coefficient.T, cross_total, precision=precise), coefficient, precision=precise
    )
    update_cols = jnp.einsum(
        "cub,bd->cud", image_cols, coefficient, precision=precise
    ) - 0.5 * jnp.einsum("cub,bd->cud", vec_cols, middle, precision=precise)
    update_rows = column_to_rows(update_cols)
    symmetric = jnp.where(
        strict, matrix, jnp.where(on_diag, 0.5 * (matrix + jnp.swapaxes(matrix, 1, 3)), 0.0)
    )
    fresh = (
        symmetric
        - jnp.einsum("rtb,cub->rtcu", update_rows, vec_cols, precision=precise)
        - jnp.einsum("rtb,cub->rtcu", vec_rows, update_cols, precision=precise)
    )
    return jnp.where(jnp.logical_or(strict, on_diag), fresh, 0.0)


def solution(mesh):
    placed = (P(None, "prow", None, "pcol"), P(None, "prow", None))
    return jax.shard_map(
        body, mesh=mesh, in_specs=placed, out_specs=P(None, "prow", None, "pcol"), check_vma=False
    )
```

profile of v0, /device:TPU:1, one launch (start us, length us, event | category | flops | bytes accessed | tf_op | source)
XLA Modules:
  0.0 1011.6 jit_solution(3026105231130807556)
XLA Ops:
  6.5 1.9 select_bitcast_fusion.3
  8.5 242.7 %all-reduce.15.cloned.1.call-done = (f32[1,1,256,256]{3,2,1,0:T(8,128)}, f32[1,1,256,256]{3,2,1,0:T(8,128)}) async-done(((f32[1,1,256,256]{3,2,1,0:T(8,128)}, f32[1,1,256,256]{3,2,1,0:T(8,128)}), (f32[1,1,256,256]{3,2,1,0:T(8,128)}, f32[1,1,256,256]{3,2,1,0:T(8,128)})) %all-reduce.15.cloned.1.call-update) | async-done | bytes 524304 | tf_op jit(solution)/shard_map/psum | solution.py:11
  251.2 2.4 convolution_bitcast_fusion.5
  253.6 0.9 copy-done.7
  254.5 1.9 fusion.6
  256.4 165.1 %all-reduce.9.cloned.1.call-done = f32[1,256,256]{2,1,0:T(8,128)} async-done(((f32[1,256,256]{2,1,0:T(8,128)}), f32[1,256,256]{2,1,0:T(8,128)}) %all-reduce.9.cloned.1.call-update) | async-done | bytes 262160 | tf_op jit(solution)/shard_map/psum | solution.py:68
  421.5 1.8 select_bitcast_fusion.1
  423.4 0.9 copy-done
  424.3 1.7 convolution_bitcast_fusion.4
  426.0 236.9 %all-reduce.13.cloned.1.call-done = (f32[2,256,256]{2,1,0:T(8,128)}, f32[1,1,256,256]{3,2,1,0:T(8,128)}, f32[1,1,256,256]{3,2,1,0:T(8,128)}) async-done(((f32[2,256,256]{2,1,0:T(8,128)}, f32[1,1,256,256]{3,2,1,0:T(8,128)}, f32[1,1,256,256]{3,2,1,0:T(8,128)}), (f32[2,256,256]{2,1,0:T(8,128)}, f32[1,1,256,256]{3,2,1,0:T(8,128)}, f32[1,1,256,256]{3,2,1,0:T(8,128)})) %all-reduce.13.cloned.1.call-update) | async-done | bytes 1048592 | tf_op jit(solution)/shard_map/psum | solution.py:69
  662.9 2.9 convolution_bitcast_fusion.3
  666.1 168.6 %all-reduce.17.cloned.1.call-done = (f32[256,256]{1,0:T(8,128)}, f32[256,256]{1,0:T(8,128)}) async-done(((f32[256,256]{1,0:T(8,128)}, f32[256,256]{1,0:T(8,128)}), (f32[256,256]{1,0:T(8,128)}, f32[256,256]{1,0:T(8,128)})) %all-reduce.17.cloned.1.call-update) | async-done | bytes 524304 | tf_op jit(solution)/shard_map/psum | solution.py:73
  834.8 2.6 gather_fusion
  837.4 0.5 fusion.48
  837.9 0.4 fusion.12
  844.0 0.5 copy-done.4
  844.6 0.6 fusion.22
  845.6 0.6 fusion.60
  846.6 0.6 fusion
  847.2 0.7 fusion.20
  848.2 0.7 convolution_bitcast_fusion
  848.8 153.4 %all-reduce.11.cloned.1.call-done = f32[256,256]{1,0:T(8,128)} async-done(((f32[256,256]{1,0:T(8,128)}), f32[256,256]{1,0:T(8,128)}) %all-reduce.11.cloned.1.call-update) | async-done | bytes 262160 | tf_op jit(solution)/shard_map/psum | solution.py:11
  1002.2 1.6 fusion.3
  1003.9 1.2 copy.18
  (44 shorter events, 7.1 us)
Async XLA Ops:
  6.5 244.6 %all-reduce.15.cloned.1.call-start = ((), (), s32[]{:S(2)}) async-start(), calls=%async_computation.3 | async-start | bytes 1048576 | tf_op jit(solution)/shard_map/psum | solution.py:11
  6.5 244.6 %copy-start.2 = (f32[1,256,2,256]{3,2,1,0:T(2,128)S(1)}, f32[1,256,2,256]{3,2,1,0:T(2,128)}, u32[]{:S(2)}) copy-start(f32[1,256,2,256]{3,2,1,0:T(2,128)} %param.2) | copy-start | bytes 1572868
  8.4 413.1 %all-reduce.9.cloned.1.call-start = ((), (), s32[]{:S(2)}) async-start(), calls=%async_computation | async-start | bytes 524288 | tf_op jit(solution)/shard_map/psum | solution.py:68
  253.5 0.9 copy-start.7
  253.6 409.4 %all-reduce.13.cloned.1.call-start = ((), (), s32[]{:S(2)}) async-start(), calls=%async_computation.2 | async-start | bytes 2097152 | tf_op jit(solution)/shard_map/psum | solution.py:69
  423.3 0.9 copy-start
  423.3 1.0 copy-start.1
  423.3 411.4 %all-reduce.17.cloned.1.call-start = ((), (), s32[]{:S(2)}) async-start(), calls=%async_computation.4 | async-start | bytes 1048576 | tf_op jit(solution)/shard_map/psum | solution.py:73
  665.9 336.4 %all-reduce.11.cloned.1.call-start = ((), (), s32[]{:S(2)}) async-start(), calls=%async_computation.1 | async-start | bytes 524288 | tf_op jit(solution)/shard_map/psum | solution.py:11
  834.8 2.6 copy-start.3
  843.1 1.0 copy-start.6
  843.5 1.1 copy-start.4
  843.5 1.1 copy-start.5
  844.6 0.9 copy-start.8
Sparse Core Ops, SparseCore 0:
  10.3 240.8 all-reduce.14
  254.3 167.1 all-reduce.8
  424.6 238.3 all-reduce.12
  666.0 168.6 all-reduce.16
  848.1 154.1 all-reduce.10
where the time goes:
time: 1010 us
  waiting for transfers between devices  967 us (96%)
  matrix products  19.7 us (2%)
  between operations  13.4 us (1%)
    psum x2, waiting for transfers between devices, spread(): return lax.psum(jnp.where(mine, shard, jnp.zeros_like(shard)), axis)  396 us
    psum x1, waiting for transfers between devices, body(): sums_cols = lax.psum(part_cols, 'prow')  237 us
    psum x1, waiting for transfers between devices, body(): gram_total, cross_total = lax.psum((gram_part, cross_part), 'pcol')  169 us
    psum x1, waiting for transfers between devices, body(): sums_rows = lax.psum(part_rows, 'pcol')  165 us
  transfers between devices with their start and end apart: 5, of which 5 were waited for; matrix products, arithmetic and copies ran while one was open for 0% of the time, Pallas kernels for 0%

commit v1 on v0

v1 whole, which is shorter than its diff:
```python
import jax
import jax.numpy as jnp
from jax import lax
from jax.experimental import pallas as pl
from jax.experimental.pallas import tpu as pltpu
from jax.sharding import PartitionSpec as P

MESH = pl.DeviceIdType.MESH
f32 = jnp.float32
NP, NQ, T, S = 32, 16, 256, 16
Z = 16


def dot(a, b, ca=1, cb=0):
    return lax.dot_general(a, b, (((ca,), (cb,)), ((), ())), precision=lax.Precision.HIGHEST, preferred_element_type=f32)


def copy_to(src, dst, send_sem, recv_sem, p, q):
    return pltpu.make_async_remote_copy(
        src_ref=src, dst_ref=dst, send_sem=send_sem, recv_sem=recv_sem, device_id=(p, q), device_id_type=MESH
    )


def loop(lo, hi, fn):
    def step(i, carry):
        fn(i)
        return carry

    lax.fori_loop(lo, hi, step, 0)


def rows(ref, i, n=S):
    return ref.at[pl.ds(pl.multiple_of(i * n, n), n)]


def kernel(a_ref, r_ref, o_ref, vp, vc, low, pc, colbuf, accbuf, rowbuf, rpart, wsl, wp, wc, gfull, gs, gy, gz, gram,
           mpart, mswap, mh, mrs, ms, mz, mtot, stack, coef, yp, yc, gmat,
           v_s, v_r, c1_s, c1_r, c2_s, c2_r, row_s, row_r, wr_s, wr_r, wcol_s, wcol_r, gz_s, gz_r, ga_s, ga_r,
           sw_s, sw_r, mr_s, mr_r, mz_s, mz_r, ma_s, ma_r):
    p = lax.axis_index("prow")
    q = lax.axis_index("pcol")
    y = p // Z
    z = lax.rem(p, Z)
    core = lax.rem(q, 2)
    mate = q + 1 - 2 * core
    chip = y * 8 + q // 2
    far = (4, 8, 12)
    near = (15, 1, 2)
    last_q = jnp.minimum(p, NQ - 1)

    def plane_row(yy):
        return yy * Z + z

    def up(d):
        return y * Z + lax.rem(z + d, Z)

    barrier = pltpu.get_barrier_semaphore()

    def greet(pp, qq):
        pl.semaphore_signal(barrier, inc=1, device_id=(pp, qq), device_id_type=MESH)

    def greet_sources(j):
        for h in range(2):
            @pl.when(q + h * NQ < p)
            def _():
                greet(q + h * NQ, j)

    loop(0, NQ, greet_sources)
    loop(1, NP, lambda d: greet(lax.rem(p + d, NP), q))
    loop(1, NQ, lambda d: greet(p, lax.rem(q + d, NQ)))
    loop(0, 8, lambda i: greet(plane_row(1 - y), 2 * i + core))

    raw = r_ref[...]
    ii = lax.broadcasted_iota(jnp.int32, (T, T), 0)
    jj = lax.broadcasted_iota(jnp.int32, (T, T), 1)
    unit = jnp.where(ii > jj, raw, jnp.where(ii == jj, 1.0, 0.0))
    vec = jnp.where(p == 0, 0.0, jnp.where(p == 1, unit, raw))
    vp[...] = vec
    gfull[...] = dot(vec, vec, 0, 0)
    gs[0] = gfull[pl.ds(pl.multiple_of(q * S, S), S), :]
    for h in range(2):
        c = q + h * NQ

        @pl.when(c <= p)
        def _():
            tile = a_ref[:, h, :] * jnp.where(c < p, 1.0, 0.5)
            low[h] = tile
            pc[h] = dot(tile, vp[...], 0, 0)

        @pl.when(c == p)
        def _():
            vc[h] = vp[...]

    pl.semaphore_wait(barrier, (NP - 1 - p) + (NP - 1) + (NQ - 1) + 8)

    def v_copy(pp):
        return copy_to(rows(vp, q), rows(vc.at[y], q), v_s.at[pp], v_r.at[y], pp, z)

    loop(p + 1, NP, lambda pp: v_copy(pp).start())

    def gram_copy(k, stage, dst, pp):
        return copy_to(gs.at[stage], dst, gz_s.at[k], gz_r.at[k], pp, q)

    gy_copy = gram_copy(0, 0, gy, plane_row(1 - y))
    gy_copy.start()

    def c1_copy(h, j):
        return copy_to(rows(pc.at[h], j), colbuf.at[q + h * NQ], c1_s.at[h, j], c1_r.at[q + h * NQ], p, j)

    for h in range(2):
        @pl.when(q + h * NQ <= p)
        def _():
            def send(d):
                c1_copy(h, lax.rem(q + d, NQ)).start()

            loop(1, NQ, send)
            colbuf[q + h * NQ] = pc[h, pl.ds(pl.multiple_of(q * S, S), S), :]

    gy_copy.wait_recv()
    gs[1] = gs[0] + gy[...]
    g1 = [gram_copy(1 + k, 1, gz.at[k], up(d)) for k, d in enumerate(far)]
    for c in g1:
        c.start()

    def c2_copy(c):
        return copy_to(colbuf.at[c], accbuf.at[p], c2_s.at[c], c2_r.at[p], c, q)

    def c1_wait(c):
        @pl.when(lax.rem(c, NQ) != q)
        def _():
            copy_to(colbuf.at[c], colbuf.at[c], c1_s.at[0, 0], c1_r.at[c], p, q).wait_recv()

    def pass_on(c):
        c1_wait(c)
        c2_copy(c).start()

    loop(0, p, pass_on)
    c1_wait(p)

    for c in g1:
        c.wait_recv()
    gs[2] = (gs[1] + gz[0]) + (gz[1] + gz[2])
    g2 = [gram_copy(4 + k, 2, gz.at[3 + k], up(d)) for k, d in enumerate(near)]
    for c in g2:
        c.start()

    for h in range(2):
        @pl.when(q + h * NQ < p)
        def _():
            copy_to(vc.at[h], vc.at[h], v_s.at[0], v_r.at[h], p, q).wait_recv()

    @pl.when(q <= p)
    def _():
        rpart[...] = dot(low[0], vc[0])

    @pl.when(q + NQ <= p)
    def _():
        rpart[...] += dot(low[1], vc[1])

    def row_copy(j):
        return copy_to(rows(rpart, j), rowbuf.at[q], row_s.at[j], row_r.at[q], p, j)

    @pl.when(q <= p)
    def _():
        loop(1, NQ, lambda d: row_copy(lax.rem(q + d, NQ)).start())
        rowbuf[q] = rpart[pl.ds(pl.multiple_of(q * S, S), S), :]

    mpart[...] = jnp.zeros_like(mpart)
    for h in range(2):
        @pl.when(q + h * NQ <= p)
        def _():
            mpart[...] += dot(pc[h], vc[h], 0, 0)

    half = T // 2
    swap1 = copy_to(rows(mpart, 1 - core, half), mswap, sw_s.at[0], sw_r.at[0], p, mate)
    swap1.start()

    for c in g2:
        c.wait_recv()
    gs[3] = (gs[2] + gz[3]) + (gz[4] + gz[5])
    gram[pl.ds(pl.multiple_of(q * S, S), S), :] = gs[3]

    def gall_copy(j):
        return copy_to(gs.at[3], rows(gram, q), ga_s.at[j], ga_r.at[q], p, j)

    loop(1, NQ, lambda d: gall_copy(lax.rem(q + d, NQ)).start())

    swap1.wait_recv()
    mh[...] = mpart[pl.ds(pl.multiple_of(core * half, half), half), :] + mswap[...]

    def mr_copy(i):
        return copy_to(rows(mh, i, 8), mrs.at[chip], mr_s.at[i], mr_r.at[chip], plane_row(i // 8), 2 * lax.rem(i, 8) + core)

    loop(1, 16, lambda d: mr_copy(lax.rem(chip + d, 16)).start())
    mrs[chip] = mh[pl.ds(pl.multiple_of(chip * 8, 8), 8), :]

    wsl[...] = colbuf[p]

    def row_add(j):
        @pl.when(j != q)
        def _():
            copy_to(rowbuf.at[j], rowbuf.at[j], row_s.at[0], row_r.at[j], p, q).wait_recv()

        wsl[...] += rowbuf[j]

    def col_add(pp):
        copy_to(accbuf.at[pp], accbuf.at[pp], c2_s.at[0], c2_r.at[pp], p, q).wait_recv()
        wsl[...] += accbuf[pp]

    loop(0, last_q + 1, row_add)
    loop(p + 1, NP, col_add)

    def wcol_copy(pp):
        return copy_to(wsl, rows(wc.at[y], q), wcol_s.at[pp], wcol_r.at[y], pp, z)

    def wrow_copy(j):
        return copy_to(wsl, rows(wp, q), wr_s.at[j], wr_r.at[q], p, j)

    def not_me(j, fn):
        @pl.when(j != q)
        def _():
            fn(j)

    loop(p + 1, NP, lambda pp: wcol_copy(pp).start())
    loop(0, last_q + 1, lambda j: not_me(j, lambda i: wrow_copy(i).start()))
    wp[pl.ds(pl.multiple_of(q * S, S), S), :] = wsl[...]

    ms[0] = mrs[chip]

    def mr_add(d):
        i = lax.rem(chip + d, 16)
        copy_to(mrs.at[i], mrs.at[i], mr_s.at[0], mr_r.at[i], p, q).wait_recv()
        ms[0] += mrs[i]

    loop(1, 16, mr_add)

    def mz_copy(k, stage, pp):
        return copy_to(ms.at[stage], mz.at[k], mz_s.at[k], mz_r.at[k], pp, q)

    m1 = [mz_copy(k, 0, up(d)) for k, d in enumerate(far)]
    for c in m1:
        c.start()

    def gall_wait(d):
        j = lax.rem(q + d, NQ)
        copy_to(rows(gram, j), rows(gram, j), ga_s.at[0], ga_r.at[j], p, q).wait_recv()

    loop(1, NQ, gall_wait)
    diag = jnp.where(ii == jj, 0.5 * gram[...], 0.0)
    power = jnp.where(ii < jj, -gram[...], 0.0) / jnp.sum(diag, axis=1, keepdims=True)
    stack[0:T] = jnp.where(ii == jj, 1.0, power)
    stack[T:] = dot(power, power)

    def double(_):
        both = dot(stack[...], stack[T:])
        stack[0:T] += both[0:T]
        stack[T:] = both[T:]

    loop(0, 3, double)

    for c in m1:
        c.wait_recv()
    ms[1] = (ms[0] + mz[0]) + (mz[1] + mz[2])
    m2 = [mz_copy(3 + k, 1, up(d)) for k, d in enumerate(near)]
    for c in m2:
        c.start()

    loop(0, 3, double)
    coef[...] = (stack[0:T] + dot(stack[0:T], stack[T:])) / jnp.sum(diag, axis=0, keepdims=True)

    for c in m2:
        c.wait_recv()
    ms[2] = (ms[1] + mz[3]) + (mz[4] + mz[5])

    def place(i):
        return mtot.at[pl.ds(pl.multiple_of(core * half + i * 8, 8), 8)]

    def mall_copy(i):
        return copy_to(ms.at[2], place(chip), ma_s.at[i], ma_r.at[chip], plane_row(i // 8), 2 * lax.rem(i, 8) + core)

    loop(1, 16, lambda d: mall_copy(lax.rem(chip + d, 16)).start())
    mtot[pl.ds(pl.multiple_of(core * half + chip * 8, 8), 8), :] = ms[2]

    yp[...] = dot(vp[...], coef[...], 1, 1)
    for h in range(2):
        @pl.when(q + h * NQ <= p)
        def _():
            yc[h] = dot(vc[h], coef[...], 1, 1)

    def mall_wait(d):
        i = lax.rem(chip + d, 16)
        copy_to(place(i), place(i), ma_s.at[0], ma_r.at[i], p, q).wait_recv()

    loop(1, 16, mall_wait)
    swap2 = copy_to(rows(mtot, core, half), rows(mtot, core, half), sw_s.at[1], sw_r.at[1], p, mate)
    swap2.start()
    copy_to(rows(mtot, 1 - core, half), rows(mtot, 1 - core, half), sw_s.at[1], sw_r.at[1], p, mate).wait_recv()
    swap2.wait_send()
    cross = mtot[...] + mtot[...].T
    middle = dot(dot(coef[...], cross, 0, 0), coef[...])
    gmat[...] = dot(vp[...], middle)

    @pl.when(q <= p)
    def _():
        def wr_wait(j):
            copy_to(rows(wp, j), rows(wp, j), wr_s.at[0], wr_r.at[j], p, q).wait_recv()

        loop(0, NQ, lambda j: not_me(j, wr_wait))

    for h in range(2):
        c = q + h * NQ

        @pl.when(c < p)
        def _():
            copy_to(wc.at[h], wc.at[h], wcol_s.at[0], wcol_r.at[h], p, q).wait_recv()

        @pl.when(c == p)
        def _():
            wc[h] = wp[...]

        @pl.when(c <= p)
        def _():
            tile = a_ref[:, h, :]
            sym = jnp.where(c < p, tile, 0.5 * (tile + tile.T))
            o_ref[:, h, :] = (sym - dot(wp[...], yc[h], 1, 1) - dot(yp[...], wc[h], 1, 1)) + dot(gmat[...], vc[h], 1, 1)

        @pl.when(c > p)
        def _():
            o_ref[:, h, :] = jnp.zeros((T, T), f32)

    loop(p + 1, NP, lambda pp: v_copy(pp).wait_send())
    loop(p + 1, NP, lambda pp: wcol_copy(pp).wait_send())
    loop(0, p, lambda c: c2_copy(c).wait_send())
    for h in range(2):
        @pl.when(q + h * NQ <= p)
        def _():
            loop(1, NQ, lambda d: c1_copy(h, lax.rem(q + d, NQ)).wait_send())

    @pl.when(q <= p)
    def _():
        loop(1, NQ, lambda d: row_copy(lax.rem(q + d, NQ)).wait_send())

    loop(0, last_q + 1, lambda j: not_me(j, lambda i: wrow_copy(i).wait_send()))
    loop(1, NQ, lambda d: gall_copy(lax.rem(q + d, NQ)).wait_send())
    loop(1, 16, lambda d: mr_copy(lax.rem(chip + d, 16)).wait_send())
    loop(1, 16, lambda d: mall_copy(lax.rem(chip + d, 16)).wait_send())
    for c in [gy_copy, swap1] + g1 + g2 + m1 + m2:
        c.wait_send()


def body(matrix, reflectors):
    vmem = lambda *shape: pltpu.VMEM(shape, f32)
    dma = lambda *shape: pltpu.SemaphoreType.DMA(shape)
    out = pl.pallas_call(
        kernel,
        out_shape=jax.ShapeDtypeStruct((T, 2, T), f32),
        in_specs=[pl.BlockSpec(memory_space=pltpu.VMEM)] * 2,
        out_specs=pl.BlockSpec(memory_space=pltpu.VMEM),
        scratch_shapes=[
            vmem(T, T), vmem(2, T, T), vmem(2, T, T), vmem(2, T, T),
            vmem(NP, S, T), vmem(NP, S, T), vmem(NQ, S, T),
            vmem(T, T), vmem(S, T), vmem(T, T), vmem(2, T, T),
            vmem(T, T), vmem(4, S, T), vmem(S, T), vmem(6, S, T), vmem(T, T),
            vmem(T, T), vmem(T // 2, T), vmem(T // 2, T), vmem(16, 8, T), vmem(3, 8, T), vmem(6, 8, T), vmem(T, T),
            vmem(2 * T, T), vmem(T, T), vmem(T, T), vmem(2, T, T), vmem(T, T),
            dma(NP), dma(2), dma(2, NQ), dma(NP), dma(NP), dma(NP), dma(NQ), dma(NQ), dma(NQ), dma(NQ), dma(NP), dma(2),
            dma(7), dma(7), dma(NQ), dma(NQ),
            dma(2), dma(2), dma(16), dma(16), dma(6), dma(6), dma(16), dma(16),
        ],
        compiler_params=pltpu.CompilerParams(collective_id=0, has_side_effects=True, vmem_limit_bytes=40 * 2**20),
        cost_estimate=pl.CostEstimate(flops=34 * 2 * T**3, bytes_accessed=5 * T * T * 4, transcendentals=0),
    )(matrix.reshape(T, 2, T), reflectors.reshape(T, T))
    return out.reshape(matrix.shape)


def solution(mesh):
    placed = (P(None, "prow", None, "pcol"), P(None, "prow", None))
    return jax.shard_map(
        body, mesh=mesh, in_specs=placed, out_specs=P(None, "prow", None, "pcol"), check_vma=False
    )
```

time: 1010 us -> 101 us (0.10)
  waiting for transfers between devices: 967 us -> 0 us
  Pallas kernels: 0 us -> 98.2 us
  matrix products: 19.7 us -> 0 us
  between operations: 13.4 us -> 0.01 us
    psum x5 -> x0, waiting for transfers between devices: 967 us -> none  [the longest x2 396 us: spread(): return lax.psum(jnp.where(mine, shard, jnp.zeros_like(shard)), axis)]
    pallas_call x0 -> x1, Pallas kernels: none -> 98.2 us  [body(): pl.pallas_call(kernel, out_shape=jax.ShapeDtypeStruct((T, 2, T), f32), in...]
    dot_general x26 -> x0, matrix products: 19.7 us -> none  [the longest x8 3.22 us: invert_factor(): result = jnp.dot(result, eye_matrix + power, precision=precise)]
  transfers between devices with their start and end apart: 5 -> 0, of which waited for: 5 -> 0; matrix products, arithmetic and copies ran while one was open for 0% -> 0% of each run, Pallas kernels for 0% -> 0%
where the time goes in v1:
time: 101 us
  Pallas kernels  98.2 us (97%)
  local copies, waits for them, and re-layouts  2.79 us (3%)
    pallas_call x1, Pallas kernels, body(): pl.pallas_call(kernel, out_shape=jax.ShapeDtypeStruct((T, 2, T), f32), in...  98.2 us
    unnamed x5, local copies, waits for them, and re-layouts  2.79 us

profile of v1, /device:TPU:1, one launch (start us, length us, event | category | flops | bytes accessed | tf_op | source)
XLA Modules:
  0.0 101.0 jit_solution(8577672190202706158)
XLA Ops:
  0.0 0.0 copy-start
  0.0 1.0 %copy-done = f32[1,256,2,256]{3,2,1,0:T(2,128)S(1)} copy-done((f32[1,256,2,256]{3,2,1,0:T(2,128)S(1)}, f32[1,256,2,256]{3,2,1,0:T(2,128)}, u32[]{:S(2)}) %copy-start) | copy-done | bytes 524312
  1.0 0.0 copy-start.1
  1.0 0.9 copy-done.1
  2.0 98.2 %shard_map.28 = f32[256,2,256]{2,1,0:T(2,128)S(1)} custom-call(f32[256,2,256]{2,1,0:T(2,128)S(1)} %bitcast.4, f32[256,256]{1,0:T(8,128)S(1)} %bitcast.5), custom_call_target="tpu_custom_call" | custom-call | flops 1140850688 | bytes 1310720 | tf_op jit(solution)/shard_map/pallas_call | solution.py:354
  100.2 0.8 copy.4
Async XLA Ops:
  0.0 1.0 %copy-start = (f32[1,256,2,256]{3,2,1,0:T(2,128)S(1)}, f32[1,256,2,256]{3,2,1,0:T(2,128)}, u32[]{:S(2)}) copy-start(f32[1,256,2,256]{3,2,1,0:T(2,128)} %param.2) | copy-start | bytes 1572868
  1.0 0.9 copy-start.1

commit v2 on v1

v2 whole, which is shorter than its diff:
```python
import jax
import jax.numpy as jnp
from jax import lax
from jax.experimental import pallas as pl
from jax.experimental.pallas import tpu as pltpu
from jax.sharding import PartitionSpec as P

MESH = pl.DeviceIdType.MESH
f32 = jnp.float32
NP, NQ, T, S = 32, 16, 256, 16
Z = 16
FAR = 5


def dot(a, b, ca=1, cb=0):
    return lax.dot_general(a, b, (((ca,), (cb,)), ((), ())), precision=lax.Precision.HIGHEST, preferred_element_type=f32)


def copy_to(src, dst, send_sem, recv_sem, p, q):
    return pltpu.make_async_remote_copy(
        src_ref=src, dst_ref=dst, send_sem=send_sem, recv_sem=recv_sem, device_id=(p, q), device_id_type=MESH
    )


def loop(lo, hi, fn):
    def step(i, carry):
        fn(i)
        return carry

    lax.fori_loop(lo, hi, step, 0)


def rows(ref, i, n=S):
    return ref.at[pl.ds(pl.multiple_of(i * n, n), n)]


def kernel(a_hbm, r_hbm, o_ref, a_ref, r_ref, vp, vc, low, pc, cbuf, abuf, rowbuf, rpart, wsl, wp, wc, vrel, wrel,
           gs, gx, gram, ms, mx, mtot, stack, coef, lhs, rhs,
           in_s, v_s, v_r, vf_s, vf_r, w_s, w_r, wf_s, wf_r, c1_s, c1_r, c2_s, c2_r, row_s, row_r, wr_s, wr_r,
           gx_s, gx_r, ga_s, ga_r, mx_s, mx_r, ma_s, ma_r):
    p = lax.axis_index("prow")
    q = lax.axis_index("pcol")
    y = p // Z
    z = lax.rem(p, Z)
    last_q = jnp.minimum(p, NQ - 1)
    get_r = pltpu.make_async_copy(r_hbm, r_ref, in_s.at[0])
    get_a = pltpu.make_async_copy(a_hbm, a_ref, in_s.at[1])
    get_r.start()
    get_a.start()

    def plane(d):
        return lax.rem(z + d + Z, Z)

    def not_me(j, fn):
        @pl.when(j != q)
        def _():
            fn(j)

    def source(k):
        return plane((0, -FAR, FAR)[k]), (5, 6, 5)[k]

    def targets(k, fn):
        t, n = source(k)

        def one(i):
            yy = lax.rem(i, 2)
            pp = yy * Z + plane(i // 2 - 2)
            fn(i, pp, t, pp > y * Z + t, (pp == p) & (t == q))

        loop(0, 2 * n, one)

    barrier = pltpu.get_barrier_semaphore()

    def greet(pp, qq):
        pl.semaphore_signal(barrier, inc=1, device_id=(pp, qq), device_id_type=MESH)

    off = lax.rem(z - q + 7 + Z, Z) - 7
    step = jnp.where(off < -2, -FAR, jnp.where(off > 2, FAR, 0))
    from_z = lax.rem(q + step + Z, Z)
    for h in range(2):
        @pl.when(q + h * NQ < p)
        def _():
            def hello(j):
                @pl.when((h != y) | (from_z != z) | (j != q))
                def _():
                    greet(h * Z + from_z, j)

            loop(0, NQ, hello)

    loop(1, Z, lambda d: greet(y * Z + plane(d), q))
    loop(1, 4, lambda d: greet((1 - y) * Z + plane(4 * d), q))
    loop(1, NQ, lambda d: greet(p, lax.rem(q + d, NQ)))
    loop(0, NQ, lambda j: greet((1 - y) * Z + z, j))
    count = jnp.int32(18 + 31)
    for k in range(3):
        t, n = source(k)
        for i in range(2 * n):
            pp = (i % 2) * Z + plane(i // 2 - 2)
            count += ((pp > y * Z + t) & ((pp != p) | (t != q))).astype(jnp.int32)

    get_r.wait()
    raw = r_ref[...]
    ii = lax.broadcasted_iota(jnp.int32, (T, T), 0)
    jj = lax.broadcasted_iota(jnp.int32, (T, T), 1)
    unit = jnp.where(ii > jj, raw, jnp.where(ii == jj, 1.0, 0.0))
    vp[...] = jnp.where(p == 0, 0.0, jnp.where(p == 1, unit, raw)).T
    gs[0] = dot(vp[pl.ds(pl.multiple_of(q * S, S), S), :], vp[...], 1, 1)
    get_a.wait()
    for h in range(2):
        c = q + h * NQ

        @pl.when(c <= p)
        def _():
            tile = a_ref[:, h, :] * jnp.where(c < p, 1.0, 0.5)
            low[h] = tile
            pc[h] = dot(vp[...], tile)

        @pl.when(c == p)
        def _():
            vc[h] = vp[...]

    pl.semaphore_wait(barrier, count)

    def first(src, rel, f_s, f_r):
        return [
            copy_to(src, rel.at[0], f_s.at[0], f_r.at[0], y * Z + plane(FAR), q),
            copy_to(src, rel.at[1], f_s.at[1], f_r.at[1], y * Z + plane(-FAR), q),
        ]

    def fan(k, src, dst, s_s, s_r):
        def send(i, pp, t, live, me):
            @pl.when(live & jnp.logical_not(me))
            def _():
                copy_to(src, rows(dst.at[y], q), s_s.at[k, i], s_r.at[y], pp, t).start()

            @pl.when(live & me)
            def _():
                pltpu.make_async_copy(src, rows(dst.at[y], q), s_r.at[y]).start()

        targets(k, send)

    def fan_done(k, src, dst, s_s, s_r):
        def done(i, pp, t, live, me):
            @pl.when(live & jnp.logical_not(me))
            def _():
                copy_to(src, rows(dst.at[y], q), s_s.at[k, i], s_r.at[y], pp, t).wait_send()

        targets(k, done)

    v_mine = rows(vp, q)
    v_first = first(v_mine, vrel, vf_s, vf_r)
    for c in v_first:
        c.start()
    fan(0, v_mine, vc, v_s, v_r)

    def c1_copy(h, j):
        return copy_to(rows(pc.at[h], j), cbuf.at[y, q], c1_s.at[h, j], c1_r.at[y, q], h * Z + z, j)

    def c1_each(h, fn):
        def one(d):
            j = lax.rem(q + d, NQ)

            @pl.when((h != y) | (j != q))
            def _():
                fn(c1_copy(h, j))

        loop(0, NQ, one)

    for h in range(2):
        @pl.when(q + h * NQ <= p)
        def _():
            c1_each(h, lambda c: c.start())

            @pl.when(h == y)
            def _():
                cbuf[y, q] = pc[h, pl.ds(pl.multiple_of(q * S, S), S), :]

    def sum_far(buf, got, s, r):
        out = []
        for k in range(7):
            d, other = (k + 1) // 2 * 4, (k + 1) % 2
            yy = 1 - y if other else y
            out.append(copy_to(buf.at[0], got.at[k], s.at[k], r.at[k], yy * Z + plane(d), q))
        return out

    def sum_near(buf, got, s, r):
        return [
            copy_to(buf.at[1], got.at[7 + k], s.at[7 + k], r.at[7 + k], y * Z + plane(d), q)
            for k, d in enumerate((-1, 1, 2))
        ]

    def sum_far_end(copies, buf, got):
        total = buf[0]
        for k, c in enumerate(copies):
            c.wait_recv()
            total += got[k]
        buf[1] = total

    def sum_near_end(copies, buf, got):
        total = buf[1]
        for k, c in enumerate(copies):
            c.wait_recv()
            total += got[7 + k]
        buf[2] = total

    def all_copy(buf, dst, s, r, j):
        return copy_to(buf.at[2], rows(dst, q), s.at[j], r.at[q], p, j)

    def all_send(buf, dst, s, r):
        loop(1, NQ, lambda d: all_copy(buf, dst, s, r, lax.rem(q + d, NQ)).start())
        dst[pl.ds(pl.multiple_of(q * S, S), S), :] = buf[2]

    def all_wait(dst, s, r):
        def one(j):
            copy_to(rows(dst, j), rows(dst, j), s.at[0], r.at[j], p, q).wait_recv()

        loop(0, NQ, lambda j: not_me(j, one))

    g_far = sum_far(gs, gx, gx_s, gx_r)
    for c in g_far:
        c.start()

    def relay(k, rel, f_s, f_r, dst, s_s, s_r):
        copy_to(rel.at[k - 1], rel.at[k - 1], f_s.at[k - 1], f_r.at[k - 1], p, q).wait_recv()
        fan(k, rel.at[k - 1], dst, s_s, s_r)

    for k in (1, 2):
        relay(k, vrel, vf_s, vf_r, vc, v_s, v_r)

    def c1_wait(yy, i):
        @pl.when((yy != y) | (i != q))
        def _():
            copy_to(cbuf.at[yy, i], cbuf.at[yy, i], c1_s.at[0, 0], c1_r.at[yy, i], p, q).wait_recv()

    def c2_copy(i):
        return copy_to(cbuf.at[1, i], abuf.at[z], c2_s.at[i], c2_r.at[z], y * Z + i, q)

    def c2_each(fn):
        def one(k):
            size = 8 - (k + 1) // 2
            i = plane(jnp.where(lax.rem(k, 2) == 1, size, -size))

            @pl.when((y == 0) | (i <= z))
            def _():
                fn(i)

        loop(0, Z, one)

    def c2_send(i):
        c1_wait(1, i)

        @pl.when((y == 0) & (i <= z))
        def _():
            c1_wait(0, i)
            cbuf[1, i] += cbuf[0, i]

        @pl.when(i != z)
        def _():
            c2_copy(i).start()

    c2_each(c2_send)

    sum_far_end(g_far, gs, gx)
    g_near = sum_near(gs, gx, gx_s, gx_r)
    for c in g_near:
        c.start()

    for h in range(2):
        @pl.when(q + h * NQ < p)
        def _():
            copy_to(vc.at[h], vc.at[h], v_s.at[0, 0], v_r.at[h], p, q).wait_recv()

    @pl.when(q <= p)
    def _():
        rpart[...] = dot(vc[0], low[0], 1, 1)

    @pl.when(q + NQ <= p)
    def _():
        rpart[...] += dot(vc[1], low[1], 1, 1)

    def row_copy(j):
        return copy_to(rows(rpart, j), rowbuf.at[q], row_s.at[j], row_r.at[q], p, j)

    @pl.when(q <= p)
    def _():
        loop(1, NQ, lambda d: row_copy(lax.rem(q + d, NQ)).start())
        rowbuf[q] = rpart[pl.ds(pl.multiple_of(q * S, S), S), :]

    sum_near_end(g_near, gs, gx)
    all_send(gs, gram, ga_s, ga_r)

    wsl[...] = cbuf[1, z]

    def col_add(i):
        @pl.when((i != z) & ((y == 0) | (i > z)))
        def _():
            copy_to(abuf.at[i], abuf.at[i], c2_s.at[0], c2_r.at[i], p, q).wait_recv()
            wsl[...] += abuf[i]

    loop(0, Z, col_add)
    ms[0] = dot(wsl[...], vp[...], 1, 1)
    m_far = sum_far(ms, mx, mx_s, mx_r)
    for c in m_far:
        c.start()

    def row_add(j):
        @pl.when(j != q)
        def _():
            copy_to(rowbuf.at[j], rowbuf.at[j], row_s.at[0], row_r.at[j], p, q).wait_recv()

        wsl[...] += rowbuf[j]

    loop(0, last_q + 1, row_add)
    w_first = first(wsl, wrel, wf_s, wf_r)
    for c in w_first:
        c.start()
    fan(0, wsl, wc, w_s, w_r)

    def wrow_copy(j):
        return copy_to(wsl, rows(wp, q), wr_s.at[j], wr_r.at[q], p, j)

    loop(0, last_q + 1, lambda j: not_me(j, lambda i: wrow_copy(i).start()))
    wp[pl.ds(pl.multiple_of(q * S, S), S), :] = wsl[...]

    all_wait(gram, ga_s, ga_r)
    diag = jnp.where(ii == jj, 0.5 * gram[...], 0.0)
    power = jnp.where(ii < jj, -gram[...], 0.0) / jnp.sum(diag, axis=1, keepdims=True)
    stack[0:T] = jnp.where(ii == jj, 1.0, power)
    stack[T:] = dot(power, power)

    def double(_):
        both = dot(stack[...], stack[T:])
        stack[0:T] += both[0:T]
        stack[T:] = both[T:]

    loop(0, 5, double)

    for k in (1, 2):
        relay(k, wrel, wf_s, wf_r, wc, w_s, w_r)

    sum_far_end(m_far, ms, mx)
    m_near = sum_near(ms, mx, mx_s, mx_r)
    for c in m_near:
        c.start()

    double(0)
    coef[...] = (stack[0:T] + dot(stack[0:T], stack[T:])) / jnp.sum(diag, axis=0, keepdims=True)

    sum_near_end(m_near, ms, mx)
    all_send(ms, mtot, ma_s, ma_r)
    lhs[T : 2 * T] = dot(coef[...], vp[...])
    for h in range(2):
        @pl.when(q + h * NQ <= p)
        def _():
            rhs[h, 0:T] = dot(coef[...], vc[h])
            rhs[h, 2 * T :] = vc[h]

    all_wait(mtot, ma_s, ma_r)
    cross = mtot[...] + mtot[...].T
    middle = dot(dot(coef[...], cross, 0, 0), coef[...])
    lhs[2 * T :] = dot(middle, vp[...])

    @pl.when(q <= p)
    def _():
        def wr_wait(j):
            copy_to(rows(wp, j), rows(wp, j), wr_s.at[0], wr_r.at[j], p, q).wait_recv()

        loop(0, NQ, lambda j: not_me(j, wr_wait))
        lhs[0:T] = -wp[...]
        lhs[T : 2 * T] = -lhs[T : 2 * T]

    for h in range(2):
        c = q + h * NQ

        @pl.when(c < p)
        def _():
            copy_to(wc.at[h], wc.at[h], w_s.at[0, 0], w_r.at[h], p, q).wait_recv()

        @pl.when(c == p)
        def _():
            wc[h] = wp[...]

        @pl.when(c <= p)
        def _():
            rhs[h, T : 2 * T] = wc[h]
            tile = a_ref[:, h, :]
            sym = jnp.where(c < p, tile, 0.5 * (tile + tile.T))
            o_ref[:, h, :] = sym + dot(lhs[...], rhs[h], 0, 0)

        @pl.when(c > p)
        def _():
            o_ref[:, h, :] = jnp.zeros((T, T), f32)

    for k, (v_src, w_src) in enumerate(((v_mine, wsl), (vrel.at[0], wrel.at[0]), (vrel.at[1], wrel.at[1]))):
        fan_done(k, v_src, vc, v_s, v_r)
        fan_done(k, w_src, wc, w_s, w_r)
    for h in range(2):
        @pl.when(q + h * NQ <= p)
        def _():
            c1_each(h, lambda c: c.wait_send())

    def c2_sent(i):
        @pl.when(i != z)
        def _():
            c2_copy(i).wait_send()

    c2_each(c2_sent)

    @pl.when(q <= p)
    def _():
        loop(1, NQ, lambda d: row_copy(lax.rem(q + d, NQ)).wait_send())

    loop(0, last_q + 1, lambda j: not_me(j, lambda i: wrow_copy(i).wait_send()))
    loop(1, NQ, lambda d: all_copy(gs, gram, ga_s, ga_r, lax.rem(q + d, NQ)).wait_send())
    loop(1, NQ, lambda d: all_copy(ms, mtot, ma_s, ma_r, lax.rem(q + d, NQ)).wait_send())
    for c in v_first + w_first + g_far + g_near + m_far + m_near:
        c.wait_send()


def body(matrix, reflectors):
    vmem = lambda *shape: pltpu.VMEM(shape, f32)
    dma = lambda *shape: pltpu.SemaphoreType.DMA(shape)
    out = pl.pallas_call(
        kernel,
        out_shape=jax.ShapeDtypeStruct((T, 2, T), f32),
        in_specs=[pl.BlockSpec(memory_space=pltpu.HBM)] * 2,
        out_specs=pl.BlockSpec(memory_space=pltpu.VMEM),
        scratch_shapes=[
            vmem(T, 2, T), vmem(T, T),
            vmem(T, T), vmem(2, T, T), vmem(2, T, T), vmem(2, T, T),
            vmem(2, NQ, S, T), vmem(Z, S, T), vmem(NQ, S, T),
            vmem(T, T), vmem(S, T), vmem(T, T), vmem(2, T, T), vmem(2, S, T), vmem(2, S, T),
            vmem(3, S, T), vmem(10, S, T), vmem(T, T), vmem(3, S, T), vmem(10, S, T), vmem(T, T),
            vmem(2 * T, T), vmem(T, T), vmem(3 * T, T), vmem(2, 3 * T, T),
            dma(2), dma(3, 12), dma(2), dma(2), dma(2), dma(3, 12), dma(2), dma(2), dma(2),
            dma(2, NQ), dma(2, NQ), dma(Z), dma(Z), dma(NQ), dma(NQ), dma(NQ), dma(NQ),
            dma(10), dma(10), dma(NQ), dma(NQ), dma(10), dma(10), dma(NQ), dma(NQ),
        ],
        compiler_params=pltpu.CompilerParams(collective_id=0, has_side_effects=True, vmem_limit_bytes=40 * 2**20),
        cost_estimate=pl.CostEstimate(flops=34 * 2 * T**3, bytes_accessed=5 * T * T * 4, transcendentals=0),
    )(matrix.reshape(T, 2, T), reflectors.reshape(T, T))
    return out.reshape(matrix.shape)


def solution(mesh):
    placed = (P(None, "prow", None, "pcol"), P(None, "prow", None))
    return jax.shard_map(
        body, mesh=mesh, in_specs=placed, out_specs=P(None, "prow", None, "pcol"), check_vma=False
    )
```

time: 101 us -> 82.2 us (0.81)
  Pallas kernels: 98.2 us -> 79 us
    pallas_call x1, Pallas kernels: 98.2 us -> 79 us  [body(): pl.pallas_call(kernel, out_shape=jax.ShapeDtypeStruct((T, 2, T), f32), in...]
where the time goes in v2:
time: 82.2 us; the launch traced here: 81.8 us
  Pallas kernels  79 us (96%)
  local copies, waits for them, and re-layouts  2.79 us (3%)
    pallas_call x1, Pallas kernels, body(): pl.pallas_call(kernel, out_shape=jax.ShapeDtypeStruct((T, 2, T), f32), in...  79 us
    unnamed x5, local copies, waits for them, and re-layouts  2.79 us

profile of v2, /device:TPU:1, one launch (start us, length us, event | category | flops | bytes accessed | tf_op | source)
XLA Modules:
  0.0 81.8 jit_solution(2796663941419827873)
XLA Ops:
  0.0 0.0 copy-start
  0.0 1.0 %copy-done = f32[1,256,2,256]{3,2,1,0:T(2,128)S(1)} copy-done((f32[1,256,2,256]{3,2,1,0:T(2,128)S(1)}, f32[1,256,2,256]{3,2,1,0:T(2,128)}, u32[]{:S(2)}) %copy-start) | copy-done | bytes 524312
  1.0 0.0 copy-start.1
  1.0 0.9 %copy-done.1 = f32[1,256,256]{2,1,0:T(8,128)S(1)} copy-done((f32[1,256,256]{2,1,0:T(8,128)S(1)}, f32[1,256,256]{2,1,0:T(8,128)}, u32[]{:S(2)}) %copy-start.1) | copy-done | bytes 262168
  2.0 79.0 %shard_map.28 = f32[256,2,256]{2,1,0:T(2,128)S(1)} custom-call(f32[256,2,256]{2,1,0:T(2,128)S(1)} %bitcast.4, f32[256,256]{1,0:T(8,128)S(1)} %bitcast.5), custom_call_target="tpu_custom_call" | custom-call | flops 1140850688 | bytes 1310720 | tf_op jit(solution)/shard_map/pallas_call | solution.py:423
  81.0 0.8 copy.4
Async XLA Ops:
  0.0 1.0 %copy-start = (f32[1,256,2,256]{3,2,1,0:T(2,128)S(1)}, f32[1,256,2,256]{3,2,1,0:T(2,128)}, u32[]{:S(2)}) copy-start(f32[1,256,2,256]{3,2,1,0:T(2,128)} %param.2) | copy-start | bytes 1572868
  1.0 0.9 %copy-start.1 = (f32[1,256,256]{2,1,0:T(8,128)S(1)}, f32[1,256,256]{2,1,0:T(8,128)}, u32[]{:S(2)}) copy-start(f32[1,256,256]{2,1,0:T(8,128)} %param.3) | copy-start | bytes 786436

commit v3 on v2

--- a/solution.py
+++ b/solution.py
@@ -34,9 +34,9 @@
     return ref.at[pl.ds(pl.multiple_of(i * n, n), n)]
 
 
-def kernel(a_hbm, r_hbm, o_ref, a_ref, r_ref, vp, vc, low, pc, cbuf, abuf, rowbuf, rpart, wsl, wp, wc, vrel, wrel,
+def kernel(a_hbm, r_hbm, o_ref, a_ref, r_ref, vp, vc, low, pc, cbuf, nbuf, psum, abuf, rowbuf, rpart, wsl, wp, wc, vrel, wrel,
            gs, gx, gram, ms, mx, mtot, stack, coef, lhs, rhs,
-           in_s, v_s, v_r, vf_s, vf_r, w_s, w_r, wf_s, wf_r, c1_s, c1_r, c2_s, c2_r, row_s, row_r, wr_s, wr_r,
+           in_s, v_s, v_r, vf_s, vf_r, w_s, w_r, wf_s, wf_r, c1_s, c1_r, c2_s, c2_r, c3_s, c3_r, row_s, row_r, wr_s, wr_r,
            gx_s, gx_r, ga_s, ga_r, mx_s, mx_r, ma_s, ma_r):
     p = lax.axis_index("prow")
     q = lax.axis_index("pcol")
@@ -151,7 +151,6 @@
     v_first = first(v_mine, vrel, vf_s, vf_r)
     for c in v_first:
         c.start()
-    fan(0, v_mine, vc, v_s, v_r)
 
     def c1_copy(h, j):
         return copy_to(rows(pc.at[h], j), cbuf.at[y, q], c1_s.at[h, j], c1_r.at[y, q], h * Z + z, j)
@@ -174,6 +173,8 @@
             @pl.when(h == y)
             def _():
                 cbuf[y, q] = pc[h, pl.ds(pl.multiple_of(q * S, S), S), :]
+
+    fan(0, v_mine, vc, v_s, v_r)
 
     def sum_far(buf, got, s, r):
         out = []
@@ -232,21 +233,27 @@
         def _():
             copy_to(cbuf.at[yy, i], cbuf.at[yy, i], c1_s.at[0, 0], c1_r.at[yy, i], p, q).wait_recv()
 
-    def c2_copy(i):
-        return copy_to(cbuf.at[1, i], abuf.at[z], c2_s.at[i], c2_r.at[z], y * Z + i, q)
+    def group(n):
+        off = n - 7
+        k = jnp.where(off > 2, 1, jnp.where(off < -2, 2, 0))
+        a = jnp.where(off > 2, FAR, jnp.where(off < -2, -FAR, 0))
+        return plane(-off), k, a, off - a
+
+    def c2_copy(n):
+        i, k, a, b = group(n)
+        return copy_to(cbuf.at[1, i], nbuf.at[k, b + 2], c2_s.at[n], c2_r.at[k, b + 2], y * Z + plane(-b), q)
 
     def c2_each(fn):
-        def one(k):
-            size = 8 - (k + 1) // 2
-            i = plane(jnp.where(lax.rem(k, 2) == 1, size, -size))
+        def one(n):
+            i, k, a, b = group(n)
 
             @pl.when((y == 0) | (i <= z))
             def _():
-                fn(i)
+                fn(n, i, b)
 
         loop(0, Z, one)
 
-    def c2_send(i):
+    def c2_send(n, i, b):
         c1_wait(1, i)
 
         @pl.when((y == 0) & (i <= z))
@@ -254,16 +261,41 @@
             c1_wait(0, i)
             cbuf[1, i] += cbuf[0, i]
 
-        @pl.when(i != z)
-        def _():
-            c2_copy(i).start()
+        @pl.when(b != 0)
+        def _():
+            c2_copy(n).start()
 
     c2_each(c2_send)
+
+    def c3_copy(k):
+        return copy_to(psum.at[k], abuf.at[k - 1], c3_s.at[k - 1], c3_r.at[k - 1], y * Z + source(k)[0], q)
+
+    def c3_sum(k):
+        t, n = source(k)
+        psum[k] = jnp.zeros((S, T), f32)
+
+        @pl.when((y == 0) | (t <= z))
+        def _():
+            psum[k] = cbuf[1, t]
+
+        def add(i):
+            @pl.when((i != 2) & ((y == 0) | (t <= plane(i - 2))))
+            def _():
+                copy_to(nbuf.at[k, i], nbuf.at[k, i], c2_s.at[0], c2_r.at[k, i], p, q).wait_recv()
+                psum[k] += nbuf[k, i]
+
+        loop(0, n, add)
+
 
     sum_far_end(g_far, gs, gx)
     g_near = sum_near(gs, gx, gx_s, gx_r)
     for c in g_near:
         c.start()
+
+    for k in (1, 2):
+        c3_sum(k)
+        c3_copy(k).start()
+    c3_sum(0)
 
     for h in range(2):
         @pl.when(q + h * NQ < p)
@@ -289,15 +321,10 @@
     sum_near_end(g_near, gs, gx)
     all_send(gs, gram, ga_s, ga_r)
 
-    wsl[...] = cbuf[1, z]
-
-    def col_add(i):
-        @pl.when((i != z) & ((y == 0) | (i > z)))
-        def _():
-            copy_to(abuf.at[i], abuf.at[i], c2_s.at[0], c2_r.at[i], p, q).wait_recv()
-            wsl[...] += abuf[i]
-
-    loop(0, Z, col_add)
+    wsl[...] = psum[0]
+    for k in (1, 2):
+        copy_to(abuf.at[k - 1], abuf.at[k - 1], c3_s.at[0], c3_r.at[k - 1], p, q).wait_recv()
+        wsl[...] += abuf[k - 1]
     ms[0] = dot(wsl[...], vp[...], 1, 1)
     m_far = sum_far(ms, mx, mx_s, mx_r)
     for c in m_far:
@@ -333,17 +360,17 @@
         stack[0:T] += both[0:T]
         stack[T:] = both[T:]
 
-    loop(0, 5, double)
-
-    for k in (1, 2):
-        relay(k, wrel, wf_s, wf_r, wc, w_s, w_r)
+    loop(0, 4, double)
 
     sum_far_end(m_far, ms, mx)
     m_near = sum_near(ms, mx, mx_s, mx_r)
     for c in m_near:
         c.start()
 
-    double(0)
+    for k in (1, 2):
+        relay(k, wrel, wf_s, wf_r, wc, w_s, w_r)
+
+    loop(0, 2, double)
     coef[...] = (stack[0:T] + dot(stack[0:T], stack[T:])) / jnp.sum(diag, axis=0, keepdims=True)
 
     sum_near_end(m_near, ms, mx)
@@ -399,12 +426,14 @@
         def _():
             c1_each(h, lambda c: c.wait_send())
 
-    def c2_sent(i):
-        @pl.when(i != z)
-        def _():
-            c2_copy(i).wait_send()
+    def c2_sent(n, i, b):
+        @pl.when(b != 0)
+        def _():
+            c2_copy(n).wait_send()
 
     c2_each(c2_sent)
+    for k in (1, 2):
+        c3_copy(k).wait_send()
 
     @pl.when(q <= p)
     def _():
@@ -428,15 +457,15 @@
         scratch_shapes=[
             vmem(T, 2, T), vmem(T, T),
             vmem(T, T), vmem(2, T, T), vmem(2, T, T), vmem(2, T, T),
-            vmem(2, NQ, S, T), vmem(Z, S, T), vmem(NQ, S, T),
+            vmem(2, NQ, S, T), vmem(3, 6, S, T), vmem(3, S, T), vmem(2, S, T), vmem(NQ, S, T),
             vmem(T, T), vmem(S, T), vmem(T, T), vmem(2, T, T), vmem(2, S, T), vmem(2, S, T),
             vmem(3, S, T), vmem(10, S, T), vmem(T, T), vmem(3, S, T), vmem(10, S, T), vmem(T, T),
             vmem(2 * T, T), vmem(T, T), vmem(3 * T, T), vmem(2, 3 * T, T),
             dma(2), dma(3, 12), dma(2), dma(2), dma(2), dma(3, 12), dma(2), dma(2), dma(2),
-            dma(2, NQ), dma(2, NQ), dma(Z), dma(Z), dma(NQ), dma(NQ), dma(NQ), dma(NQ),
+            dma(2, NQ), dma(2, NQ), dma(Z), dma(3, 6), dma(2), dma(2), dma(NQ), dma(NQ), dma(NQ), dma(NQ),
             dma(10), dma(10), dma(NQ), dma(NQ), dma(10), dma(10), dma(NQ), dma(NQ),
         ],
-        compiler_params=pltpu.CompilerParams(collective_id=0, has_side_effects=True, vmem_limit_bytes=40 * 2**20),
+        compiler_params=pltpu.CompilerParams(collective_id=0, has_side_effects=True, vmem_limit_bytes=60 * 2**20),
         cost_estimate=pl.CostEstimate(flops=34 * 2 * T**3, bytes_accessed=5 * T * T * 4, transcendentals=0),
     )(matrix.reshape(T, 2, T), reflectors.reshape(T, T))
     return out.reshape(matrix.shape)

time: 82.2 us -> 74.5 us (0.906); the launches traced: 81.8 us -> 73.1 us
  Pallas kernels: 79 us -> 71.1 us
    pallas_call x1, Pallas kernels: 79 us -> 71.1 us  [body(): pl.pallas_call(kernel, out_shape=jax.ShapeDtypeStruct((T, 2, T), f32), in...]
    unnamed x5 -> x1, local copies, waits for them, and re-layouts: 2.79 us -> 2.01 us
where the time goes in v3:
time: 74.5 us; the launch traced here: 73.1 us
  Pallas kernels  71.1 us (95%)
  local copies, waits for them, and re-layouts  2.01 us (3%)
    pallas_call x1, Pallas kernels, body(): pl.pallas_call(kernel, out_shape=jax.ShapeDtypeStruct((T, 2, T), f32), in...  71.1 us
    unnamed x1, local copies, waits for them, and re-layouts  2.01 us

profile of v3, /device:TPU:1, one launch (start us, length us, event | category | flops | bytes accessed | tf_op | source)
XLA Modules:
  0.0 73.1 jit_solution(7402928405027221989)
XLA Ops:
  0.0 71.1 %shard_map.28 = f32[256,2,256]{2,1,0:T(2,128)} custom-call(f32[256,2,256]{2,1,0:T(2,128)} %bitcast.4, f32[256,256]{1,0:T(8,128)} %bitcast.5), custom_call_target="tpu_custom_call" | custom-call | flops 1140850688 | bytes 1310720 | tf_op jit(solution)/shard_map/pallas_call | solution.py:452
  71.1 2.0 %copy.4 = f32[1,256,2,256]{3,2,1,0:T(2,128)} copy(f32[1,256,2,256]{3,2,1,0:T(2,128)} %bitcast.3) | data formatting | bytes 1048576

commit v4 on v3

--- a/solution.py
+++ b/solution.py
@@ -34,8 +34,8 @@
     return ref.at[pl.ds(pl.multiple_of(i * n, n), n)]
 
 
-def kernel(a_hbm, r_hbm, o_ref, a_ref, r_ref, vp, vc, low, pc, cbuf, nbuf, psum, abuf, rowbuf, rpart, wsl, wp, wc, vrel, wrel,
-           gs, gx, gram, ms, mx, mtot, stack, coef, lhs, rhs,
+def kernel(a_hbm, r_hbm, o_ref, a_ref, r_ref, vp, vc, low, pc, cbuf, nbuf, psum, abuf, rowbuf, rpart, wsl, wp, vrel, wrel,
+           gs, gx, gram, ms, mx, mtot, stack, coef, yp, lhs, rhs,
            in_s, v_s, v_r, vf_s, vf_r, w_s, w_r, wf_s, wf_r, c1_s, c1_r, c2_s, c2_r, c3_s, c3_r, row_s, row_r, wr_s, wr_r,
            gx_s, gx_r, ga_s, ga_r, mx_s, mx_r, ma_s, ma_r):
     p = lax.axis_index("prow")
@@ -74,6 +74,9 @@
     def greet(pp, qq):
         pl.semaphore_signal(barrier, inc=1, device_id=(pp, qq), device_id_type=MESH)
 
+    for d in (8, FAR, -FAR):
+        greet((1 - y) * Z + plane(d), q)
+    loop(1, Z, lambda d: greet(y * Z + plane(d), q))
     off = lax.rem(z - q + 7 + Z, Z) - 7
     step = jnp.where(off < -2, -FAR, jnp.where(off > 2, FAR, 0))
     from_z = lax.rem(q + step + Z, Z)
@@ -87,8 +90,6 @@
 
             loop(0, NQ, hello)
 
-    loop(1, Z, lambda d: greet(y * Z + plane(d), q))
-    loop(1, 4, lambda d: greet((1 - y) * Z + plane(4 * d), q))
     loop(1, NQ, lambda d: greet(p, lax.rem(q + d, NQ)))
     loop(0, NQ, lambda j: greet((1 - y) * Z + z, j))
     count = jnp.int32(18 + 31)
@@ -131,11 +132,11 @@
         def send(i, pp, t, live, me):
             @pl.when(live & jnp.logical_not(me))
             def _():
-                copy_to(src, rows(dst.at[y], q), s_s.at[k, i], s_r.at[y], pp, t).start()
+                copy_to(src, dst, s_s.at[k, i], s_r.at[y], pp, t).start()
 
             @pl.when(live & me)
             def _():
-                pltpu.make_async_copy(src, rows(dst.at[y], q), s_r.at[y]).start()
+                pltpu.make_async_copy(src, dst, s_r.at[y]).start()
 
         targets(k, send)
 
@@ -143,14 +144,17 @@
         def done(i, pp, t, live, me):
             @pl.when(live & jnp.logical_not(me))
             def _():
-                copy_to(src, rows(dst.at[y], q), s_s.at[k, i], s_r.at[y], pp, t).wait_send()
+                copy_to(src, dst, s_s.at[k, i], s_r.at[y], pp, t).wait_send()
 
         targets(k, done)
 
     v_mine = rows(vp, q)
+    v_dst = rows(vc.at[y], q)
+    w_dst = rhs.at[y, pl.ds(pl.multiple_of(T + q * S, S), S)]
     v_first = first(v_mine, vrel, vf_s, vf_r)
     for c in v_first:
         c.start()
+    fan(0, v_mine, v_dst, v_s, v_r)
 
     def c1_copy(h, j):
         return copy_to(rows(pc.at[h], j), cbuf.at[y, q], c1_s.at[h, j], c1_r.at[y, q], h * Z + z, j)
@@ -174,12 +178,10 @@
             def _():
                 cbuf[y, q] = pc[h, pl.ds(pl.multiple_of(q * S, S), S), :]
 
-    fan(0, v_mine, vc, v_s, v_r)
 
     def sum_far(buf, got, s, r):
         out = []
-        for k in range(7):
-            d, other = (k + 1) // 2 * 4, (k + 1) % 2
+        for k, (d, other) in enumerate(((8, 0), (8, 1), (FAR, 0), (-FAR, 0), (FAR, 1), (-FAR, 1), (0, 1))):
             yy = 1 - y if other else y
             out.append(copy_to(buf.at[0], got.at[k], s.at[k], r.at[k], yy * Z + plane(d), q))
         return out
@@ -187,21 +189,21 @@
     def sum_near(buf, got, s, r):
         return [
             copy_to(buf.at[1], got.at[7 + k], s.at[7 + k], r.at[7 + k], y * Z + plane(d), q)
-            for k, d in enumerate((-1, 1, 2))
+            for k, d in enumerate((-2, 2, -1, 1))
         ]
 
     def sum_far_end(copies, buf, got):
         total = buf[0]
-        for k, c in enumerate(copies):
-            c.wait_recv()
+        for k in range(2, 7):
+            copies[k].wait_recv()
             total += got[k]
         buf[1] = total
 
-    def sum_near_end(copies, buf, got):
+    def sum_near_end(far, near, buf, got):
         total = buf[1]
-        for k, c in enumerate(copies):
+        for k, c in enumerate(far[:2] + near):
             c.wait_recv()
-            total += got[7 + k]
+            total += got[k if k < 2 else k + 5]
         buf[2] = total
 
     def all_copy(buf, dst, s, r, j):
@@ -226,7 +228,7 @@
         fan(k, rel.at[k - 1], dst, s_s, s_r)
 
     for k in (1, 2):
-        relay(k, vrel, vf_s, vf_r, vc, v_s, v_r)
+        relay(k, vrel, vf_s, vf_r, v_dst, v_s, v_r)
 
     def c1_wait(yy, i):
         @pl.when((yy != y) | (i != q))
@@ -234,7 +236,7 @@
             copy_to(cbuf.at[yy, i], cbuf.at[yy, i], c1_s.at[0, 0], c1_r.at[yy, i], p, q).wait_recv()
 
     def group(n):
-        off = n - 7
+        off = jnp.where(n < 6, n + 3, jnp.where(n < 11, 3 - n, n - 13))
         k = jnp.where(off > 2, 1, jnp.where(off < -2, 2, 0))
         a = jnp.where(off > 2, FAR, jnp.where(off < -2, -FAR, 0))
         return plane(-off), k, a, off - a
@@ -291,11 +293,6 @@
     g_near = sum_near(gs, gx, gx_s, gx_r)
     for c in g_near:
         c.start()
-
-    for k in (1, 2):
-        c3_sum(k)
-        c3_copy(k).start()
-    c3_sum(0)
 
     for h in range(2):
         @pl.when(q + h * NQ < p)
@@ -318,30 +315,36 @@
         loop(1, NQ, lambda d: row_copy(lax.rem(q + d, NQ)).start())
         rowbuf[q] = rpart[pl.ds(pl.multiple_of(q * S, S), S), :]
 
-    sum_near_end(g_near, gs, gx)
+    for k in (1, 2):
+        c3_sum(k)
+        c3_copy(k).start()
+
+    sum_near_end(g_far, g_near, gs, gx)
     all_send(gs, gram, ga_s, ga_r)
-
-    wsl[...] = psum[0]
-    for k in (1, 2):
-        copy_to(abuf.at[k - 1], abuf.at[k - 1], c3_s.at[0], c3_r.at[k - 1], p, q).wait_recv()
-        wsl[...] += abuf[k - 1]
+    c3_sum(0)
+
+    wsl[...] = jnp.zeros((S, T), f32)
+
+    def row_add(j):
+        @pl.when(j != q)
+        def _():
+            copy_to(rowbuf.at[j], rowbuf.at[j], row_s.at[0], row_r.at[j], p, q).wait_recv()
+
+        wsl[...] += rowbuf[j]
+
+    loop(0, last_q + 1, row_add)
     ms[0] = dot(wsl[...], vp[...], 1, 1)
     m_far = sum_far(ms, mx, mx_s, mx_r)
     for c in m_far:
         c.start()
 
-    def row_add(j):
-        @pl.when(j != q)
-        def _():
-            copy_to(rowbuf.at[j], rowbuf.at[j], row_s.at[0], row_r.at[j], p, q).wait_recv()
-
-        wsl[...] += rowbuf[j]
-
-    loop(0, last_q + 1, row_add)
+    for k in (1, 2):
+        copy_to(abuf.at[k - 1], abuf.at[k - 1], c3_s.at[0], c3_r.at[k - 1], p, q).wait_recv()
+    wsl[...] += (psum[0] + abuf[0]) + abuf[1]
     w_first = first(wsl, wrel, wf_s, wf_r)
     for c in w_first:
         c.start()
-    fan(0, wsl, wc, w_s, w_r)
+    fan(0, wsl, w_dst, w_s, w_r)
 
     def wrow_copy(j):
         return copy_to(wsl, rows(wp, q), wr_s.at[j], wr_r.at[q], p, j)
@@ -368,24 +371,19 @@
         c.start()
 
     for k in (1, 2):
-        relay(k, wrel, wf_s, wf_r, wc, w_s, w_r)
+        relay(k, wrel, wf_s, wf_r, w_dst, w_s, w_r)
 
     loop(0, 2, double)
     coef[...] = (stack[0:T] + dot(stack[0:T], stack[T:])) / jnp.sum(diag, axis=0, keepdims=True)
 
-    sum_near_end(m_near, ms, mx)
+    sum_near_end(m_far, m_near, ms, mx)
     all_send(ms, mtot, ma_s, ma_r)
-    lhs[T : 2 * T] = dot(coef[...], vp[...])
+    yp[...] = dot(coef[...], vp[...])
+    lhs[T:] = -yp[...]
     for h in range(2):
         @pl.when(q + h * NQ <= p)
         def _():
             rhs[h, 0:T] = dot(coef[...], vc[h])
-            rhs[h, 2 * T :] = vc[h]
-
-    all_wait(mtot, ma_s, ma_r)
-    cross = mtot[...] + mtot[...].T
-    middle = dot(dot(coef[...], cross, 0, 0), coef[...])
-    lhs[2 * T :] = dot(middle, vp[...])
 
     @pl.when(q <= p)
     def _():
@@ -394,33 +392,40 @@
 
         loop(0, NQ, lambda j: not_me(j, wr_wait))
         lhs[0:T] = -wp[...]
-        lhs[T : 2 * T] = -lhs[T : 2 * T]
 
     for h in range(2):
         c = q + h * NQ
 
         @pl.when(c < p)
         def _():
-            copy_to(wc.at[h], wc.at[h], w_s.at[0, 0], w_r.at[h], p, q).wait_recv()
+            copy_to(rhs.at[h, pl.ds(T, T)], rhs.at[h, pl.ds(T, T)], w_s.at[0, 0], w_r.at[h], p, q).wait_recv()
 
         @pl.when(c == p)
         def _():
-            wc[h] = wp[...]
+            rhs[h, T:] = wp[...]
 
         @pl.when(c <= p)
         def _():
-            rhs[h, T : 2 * T] = wc[h]
             tile = a_ref[:, h, :]
             sym = jnp.where(c < p, tile, 0.5 * (tile + tile.T))
-            o_ref[:, h, :] = sym + dot(lhs[...], rhs[h], 0, 0)
+            low[h] = sym + dot(lhs[...], rhs[h], 0, 0)
+
+    all_wait(mtot, ma_s, ma_r)
+    wp[...] = dot(mtot[...] + mtot[...].T, yp[...])
+    for h in range(2):
+        c = q + h * NQ
+
+        @pl.when(c <= p)
+        def _():
+            o_ref[:, h, :] = low[h] + dot(wp[...], rhs[h, 0:T], 0, 0)
 
         @pl.when(c > p)
         def _():
             o_ref[:, h, :] = jnp.zeros((T, T), f32)
 
     for k, (v_src, w_src) in enumerate(((v_mine, wsl), (vrel.at[0], wrel.at[0]), (vrel.at[1], wrel.at[1]))):
-        fan_done(k, v_src, vc, v_s, v_r)
-        fan_done(k, w_src, wc, w_s, w_r)
+        fan_done(k, v_src, v_dst, v_s, v_r)
+        fan_done(k, w_src, w_dst, w_s, w_r)
     for h in range(2):
         @pl.when(q + h * NQ <= p)
         def _():
@@ -458,12 +463,12 @@
             vmem(T, 2, T), vmem(T, T),
             vmem(T, T), vmem(2, T, T), vmem(2, T, T), vmem(2, T, T),
             vmem(2, NQ, S, T), vmem(3, 6, S, T), vmem(3, S, T), vmem(2, S, T), vmem(NQ, S, T),
-            vmem(T, T), vmem(S, T), vmem(T, T), vmem(2, T, T), vmem(2, S, T), vmem(2, S, T),
-            vmem(3, S, T), vmem(10, S, T), vmem(T, T), vmem(3, S, T), vmem(10, S, T), vmem(T, T),
-            vmem(2 * T, T), vmem(T, T), vmem(3 * T, T), vmem(2, 3 * T, T),
+            vmem(T, T), vmem(S, T), vmem(T, T), vmem(2, S, T), vmem(2, S, T),
+            vmem(3, S, T), vmem(11, S, T), vmem(T, T), vmem(3, S, T), vmem(11, S, T), vmem(T, T),
+            vmem(2 * T, T), vmem(T, T), vmem(T, T), vmem(2 * T, T), vmem(2, 2 * T, T),
             dma(2), dma(3, 12), dma(2), dma(2), dma(2), dma(3, 12), dma(2), dma(2), dma(2),
             dma(2, NQ), dma(2, NQ), dma(Z), dma(3, 6), dma(2), dma(2), dma(NQ), dma(NQ), dma(NQ), dma(NQ),
-            dma(10), dma(10), dma(NQ), dma(NQ), dma(10), dma(10), dma(NQ), dma(NQ),
+            dma(11), dma(11), dma(NQ), dma(NQ), dma(11), dma(11), dma(NQ), dma(NQ),
         ],
         compiler_params=pltpu.CompilerParams(collective_id=0, has_side_effects=True, vmem_limit_bytes=60 * 2**20),
         cost_estimate=pl.CostEstimate(flops=34 * 2 * T**3, bytes_accessed=5 * T * T * 4, transcendentals=0),

time: 74.5 us -> 76 us (1.020); the launches traced: 73.1 us -> 75.8 us
  Pallas kernels: 71.1 us -> 73.8 us
    pallas_call x1, Pallas kernels: 71.1 us -> 73.8 us  [body(): pl.pallas_call(kernel, out_shape=jax.ShapeDtypeStruct((T, 2, T), f32), in...]
where the time goes in v4:
time: 76 us; the launch traced here: 75.8 us
  Pallas kernels  73.8 us (97%)
  local copies, waits for them, and re-layouts  2.01 us (3%)
    pallas_call x1, Pallas kernels, body(): pl.pallas_call(kernel, out_shape=jax.ShapeDtypeStruct((T, 2, T), f32), in...  73.8 us
    unnamed x1, local copies, waits for them, and re-layouts  2.01 us

profile of v4, /device:TPU:1, one launch (start us, length us, event | category | flops | bytes accessed | tf_op | source)
XLA Modules:
  0.0 75.8 jit_solution(9692532610103406026)
XLA Ops:
  0.0 73.8 %shard_map.28 = f32[256,2,256]{2,1,0:T(2,128)} custom-call(f32[256,2,256]{2,1,0:T(2,128)} %bitcast.4, f32[256,256]{1,0:T(8,128)} %bitcast.5), custom_call_target="tpu_custom_call" | custom-call | flops 1140850688 | bytes 1310720 | tf_op jit(solution)/shard_map/pallas_call | solution.py:457
  73.8 2.0 %copy.4 = f32[1,256,2,256]{3,2,1,0:T(2,128)} copy(f32[1,256,2,256]{3,2,1,0:T(2,128)} %bitcast.3) | data formatting | bytes 1048576

commit v5 on v4

--- a/solution.py
+++ b/solution.py
@@ -74,7 +74,7 @@
     def greet(pp, qq):
         pl.semaphore_signal(barrier, inc=1, device_id=(pp, qq), device_id_type=MESH)
 
-    for d in (8, FAR, -FAR):
+    for d in (FAR, -FAR):
         greet((1 - y) * Z + plane(d), q)
     loop(1, Z, lambda d: greet(y * Z + plane(d), q))
     off = lax.rem(z - q + 7 + Z, Z) - 7
@@ -92,7 +92,7 @@
 
     loop(1, NQ, lambda d: greet(p, lax.rem(q + d, NQ)))
     loop(0, NQ, lambda j: greet((1 - y) * Z + z, j))
-    count = jnp.int32(18 + 31)
+    count = jnp.int32(17 + 31)
     for k in range(3):
         t, n = source(k)
         for i in range(2 * n):
@@ -179,39 +179,42 @@
                 cbuf[y, q] = pc[h, pl.ds(pl.multiple_of(q * S, S), S), :]
 
 
-    def sum_far(buf, got, s, r):
-        out = []
-        for k, (d, other) in enumerate(((8, 0), (8, 1), (FAR, 0), (-FAR, 0), (FAR, 1), (-FAR, 1), (0, 1))):
-            yy = 1 - y if other else y
-            out.append(copy_to(buf.at[0], got.at[k], s.at[k], r.at[k], yy * Z + plane(d), q))
-        return out
+    def sum_pair(buf, got, s, r):
+        return copy_to(buf.at[0], got.at[4], s.at[4], r.at[4], (1 - y) * Z + z, q)
+
+    def sum_far(buf, stage, got, s, r, pairs):
+        return [
+            copy_to(buf.at[stage], got.at[k], s.at[k], r.at[k], (1 - y if k > 1 else y) * Z + plane((FAR, -FAR)[k % 2]), q)
+            for k in range(4 if pairs else 2)
+        ]
 
     def sum_near(buf, got, s, r):
         return [
-            copy_to(buf.at[1], got.at[7 + k], s.at[7 + k], r.at[7 + k], y * Z + plane(d), q)
-            for k, d in enumerate((-2, 2, -1, 1))
+            copy_to(buf.at[3 if k == 0 else 2], got.at[5 + k], s.at[5 + k], r.at[5 + k], y * Z + plane(d), q)
+            for k, d in enumerate((-3, -2, 2, -1, 1))
         ]
 
-    def sum_far_end(copies, buf, got):
-        total = buf[0]
-        for k in range(2, 7):
-            copies[k].wait_recv()
-            total += got[k]
-        buf[1] = total
-
-    def sum_near_end(far, near, buf, got):
-        total = buf[1]
-        for k, c in enumerate(far[:2] + near):
+    def sum_far_end(copies, stage, buf, got):
+        for c in copies:
             c.wait_recv()
-            total += got[k if k < 2 else k + 5]
-        buf[2] = total
+        above = [got[k] for k in range(len(copies)) if k % 2 == 1]
+        below = [got[k] for k in range(len(copies)) if k % 2 == 0]
+        buf[2] = (buf[stage] + sum(above)) + sum(below)
+        buf[3] = sum(above)
+
+    def sum_near_end(copies, buf, got):
+        total = buf[2]
+        for k, c in enumerate(copies):
+            c.wait_recv()
+            total += got[5 + k]
+        buf[4] = total
 
     def all_copy(buf, dst, s, r, j):
-        return copy_to(buf.at[2], rows(dst, q), s.at[j], r.at[q], p, j)
+        return copy_to(buf.at[4], rows(dst, q), s.at[j], r.at[q], p, j)
 
     def all_send(buf, dst, s, r):
         loop(1, NQ, lambda d: all_copy(buf, dst, s, r, lax.rem(q + d, NQ)).start())
-        dst[pl.ds(pl.multiple_of(q * S, S), S), :] = buf[2]
+        dst[pl.ds(pl.multiple_of(q * S, S), S), :] = buf[4]
 
     def all_wait(dst, s, r):
         def one(j):
@@ -219,7 +222,11 @@
 
         loop(0, NQ, lambda j: not_me(j, one))
 
-    g_far = sum_far(gs, gx, gx_s, gx_r)
+    g_pair = sum_pair(gs, gx, gx_s, gx_r)
+    g_pair.start()
+    g_pair.wait_recv()
+    gs[1] = gs[0] + gx[4]
+    g_far = sum_far(gs, 1, gx, gx_s, gx_r, False)
     for c in g_far:
         c.start()
 
@@ -289,7 +296,7 @@
         loop(0, n, add)
 
 
-    sum_far_end(g_far, gs, gx)
+    sum_far_end(g_far, 1, gs, gx)
     g_near = sum_near(gs, gx, gx_s, gx_r)
     for c in g_near:
         c.start()
@@ -319,7 +326,7 @@
         c3_sum(k)
         c3_copy(k).start()
 
-    sum_near_end(g_far, g_near, gs, gx)
+    sum_near_end(g_near, gs, gx)
     all_send(gs, gram, ga_s, ga_r)
     c3_sum(0)
 
@@ -334,8 +341,9 @@
 
     loop(0, last_q + 1, row_add)
     ms[0] = dot(wsl[...], vp[...], 1, 1)
-    m_far = sum_far(ms, mx, mx_s, mx_r)
-    for c in m_far:
+    m_far = sum_far(ms, 0, mx, mx_s, mx_r, True)
+    m_pair = sum_pair(ms, mx, mx_s, mx_r)
+    for c in m_far + [m_pair]:
         c.start()
 
     for k in (1, 2):
@@ -365,7 +373,9 @@
 
     loop(0, 4, double)
 
-    sum_far_end(m_far, ms, mx)
+    m_pair.wait_recv()
+    ms[1] = ms[0] + mx[4]
+    sum_far_end(m_far, 1, ms, mx)
     m_near = sum_near(ms, mx, mx_s, mx_r)
     for c in m_near:
         c.start()
@@ -376,7 +386,7 @@
     loop(0, 2, double)
     coef[...] = (stack[0:T] + dot(stack[0:T], stack[T:])) / jnp.sum(diag, axis=0, keepdims=True)
 
-    sum_near_end(m_far, m_near, ms, mx)
+    sum_near_end(m_near, ms, mx)
     all_send(ms, mtot, ma_s, ma_r)
     yp[...] = dot(coef[...], vp[...])
     lhs[T:] = -yp[...]
@@ -447,7 +457,7 @@
     loop(0, last_q + 1, lambda j: not_me(j, lambda i: wrow_copy(i).wait_send()))
     loop(1, NQ, lambda d: all_copy(gs, gram, ga_s, ga_r, lax.rem(q + d, NQ)).wait_send())
     loop(1, NQ, lambda d: all_copy(ms, mtot, ma_s, ma_r, lax.rem(q + d, NQ)).wait_send())
-    for c in v_first + w_first + g_far + g_near + m_far + m_near:
+    for c in v_first + w_first + g_far + g_near + m_far + m_near + [g_pair, m_pair]:
         c.wait_send()
 
 
@@ -464,13 +474,13 @@
             vmem(T, T), vmem(2, T, T), vmem(2, T, T), vmem(2, T, T),
             vmem(2, NQ, S, T), vmem(3, 6, S, T), vmem(3, S, T), vmem(2, S, T), vmem(NQ, S, T),
             vmem(T, T), vmem(S, T), vmem(T, T), vmem(2, S, T), vmem(2, S, T),
-            vmem(3, S, T), vmem(11, S, T), vmem(T, T), vmem(3, S, T), vmem(11, S, T), vmem(T, T),
+            vmem(5, S, T), vmem(10, S, T), vmem(T, T), vmem(5, S, T), vmem(10, S, T), vmem(T, T),
             vmem(2 * T, T), vmem(T, T), vmem(T, T), vmem(2 * T, T), vmem(2, 2 * T, T),
             dma(2), dma(3, 12), dma(2), dma(2), dma(2), dma(3, 12), dma(2), dma(2), dma(2),
             dma(2, NQ), dma(2, NQ), dma(Z), dma(3, 6), dma(2), dma(2), dma(NQ), dma(NQ), dma(NQ), dma(NQ),
-            dma(11), dma(11), dma(NQ), dma(NQ), dma(11), dma(11), dma(NQ), dma(NQ),
+            dma(10), dma(10), dma(NQ), dma(NQ), dma(10), dma(10), dma(NQ), dma(NQ),
         ],
-        compiler_params=pltpu.CompilerParams(collective_id=0, has_side_effects=True, vmem_limit_bytes=60 * 2**20),
+        compiler_params=pltpu.CompilerParams(collective_id=0, has_side_effects=True, vmem_limit_bytes=53 * 2**20),
         cost_estimate=pl.CostEstimate(flops=34 * 2 * T**3, bytes_accessed=5 * T * T * 4, transcendentals=0),
     )(matrix.reshape(T, 2, T), reflectors.reshape(T, T))
     return out.reshape(matrix.shape)

time: 76 us -> 69.9 us (0.920)
  Pallas kernels: 73.8 us -> 68 us
    pallas_call x1, Pallas kernels: 73.8 us -> 68 us  [body(): pl.pallas_call(kernel, out_shape=jax.ShapeDtypeStruct((T, 2, T), f32), in...]
    unnamed x1 -> x3, local copies, waits for them, and re-layouts: 2.01 us -> 1.75 us
where the time goes in v5:
time: 69.9 us; the launch traced here: 69.8 us
  Pallas kernels  68 us (97%)
  local copies, waits for them, and re-layouts  1.75 us (3%)
    pallas_call x1, Pallas kernels, body(): pl.pallas_call(kernel, out_shape=jax.ShapeDtypeStruct((T, 2, T), f32), in...  68 us
    unnamed x3, local copies, waits for them, and re-layouts  1.75 us

profile of v5, /device:TPU:1, one launch (start us, length us, event | category | flops | bytes accessed | tf_op | source)
XLA Modules:
  0.0 69.8 jit_solution(1852027075555244720)
XLA Ops:
  0.0 0.0 copy-start
  0.0 0.9 %copy-done = f32[1,256,256]{2,1,0:T(8,128)S(1)} copy-done((f32[1,256,256]{2,1,0:T(8,128)S(1)}, f32[1,256,256]{2,1,0:T(8,128)}, u32[]{:S(2)}) %copy-start) | copy-done | bytes 262168
  1.0 68.0 %shard_map.28 = f32[256,2,256]{2,1,0:T(2,128)S(1)} custom-call(f32[256,2,256]{2,1,0:T(2,128)} %bitcast.5, f32[256,256]{1,0:T(8,128)S(1)} %bitcast.4), custom_call_target="tpu_custom_call" | custom-call | flops 1140850688 | bytes 1310720 | tf_op jit(solution)/shard_map/pallas_call | solution.py:467
  69.0 0.8 %copy.4 = f32[1,256,2,256]{3,2,1,0:T(2,128)} copy(f32[1,256,2,256]{3,2,1,0:T(2,128)S(1)} %bitcast.3) | data formatting | bytes 1048576
Async XLA Ops:
  0.0 0.9 %copy-start = (f32[1,256,256]{2,1,0:T(8,128)S(1)}, f32[1,256,256]{2,1,0:T(8,128)}, u32[]{:S(2)}) copy-start(f32[1,256,256]{2,1,0:T(8,128)} %param.3) | copy-start | bytes 786436

commit v6 on v4

--- a/solution.py
+++ b/solution.py
@@ -8,6 +8,7 @@
 MESH = pl.DeviceIdType.MESH
 f32 = jnp.float32
 NP, NQ, T, S = 32, 16, 256, 16
+H = S // 2
 Z = 16
 FAR = 5
 
@@ -35,13 +36,14 @@
 
 
 def kernel(a_hbm, r_hbm, o_ref, a_ref, r_ref, vp, vc, low, pc, cbuf, nbuf, psum, abuf, rowbuf, rpart, wsl, wp, vrel, wrel,
-           gs, gx, gram, ms, mx, mtot, stack, coef, yp, lhs, rhs,
+           gterm, gs, gx, gram, mterm, ms, mx, mtot, stack, coef, yp, lhs, rhs,
            in_s, v_s, v_r, vf_s, vf_r, w_s, w_r, wf_s, wf_r, c1_s, c1_r, c2_s, c2_r, c3_s, c3_r, row_s, row_r, wr_s, wr_r,
            gx_s, gx_r, ga_s, ga_r, mx_s, mx_r, ma_s, ma_r):
     p = lax.axis_index("prow")
     q = lax.axis_index("pcol")
     y = p // Z
     z = lax.rem(p, Z)
+    mate = q + 1 - 2 * lax.rem(q, 2)
     last_q = jnp.minimum(p, NQ - 1)
     get_r = pltpu.make_async_copy(r_hbm, r_ref, in_s.at[0])
     get_a = pltpu.make_async_copy(a_hbm, a_ref, in_s.at[1])
@@ -74,9 +76,10 @@
     def greet(pp, qq):
         pl.semaphore_signal(barrier, inc=1, device_id=(pp, qq), device_id_type=MESH)
 
-    for d in (8, FAR, -FAR):
+    for d in (FAR, -FAR):
         greet((1 - y) * Z + plane(d), q)
-    loop(1, Z, lambda d: greet(y * Z + plane(d), q))
+    for d in (FAR, -FAR, 3, 2, -2, 1, -1):
+        greet(y * Z + plane(d), q)
     off = lax.rem(z - q + 7 + Z, Z) - 7
     step = jnp.where(off < -2, -FAR, jnp.where(off > 2, FAR, 0))
     from_z = lax.rem(q + step + Z, Z)
@@ -92,7 +95,7 @@
 
     loop(1, NQ, lambda d: greet(p, lax.rem(q + d, NQ)))
     loop(0, NQ, lambda j: greet((1 - y) * Z + z, j))
-    count = jnp.int32(18 + 31)
+    count = jnp.int32(9 + 31)
     for k in range(3):
         t, n = source(k)
         for i in range(2 * n):
@@ -105,7 +108,7 @@
     jj = lax.broadcasted_iota(jnp.int32, (T, T), 1)
     unit = jnp.where(ii > jj, raw, jnp.where(ii == jj, 1.0, 0.0))
     vp[...] = jnp.where(p == 0, 0.0, jnp.where(p == 1, unit, raw)).T
-    gs[0] = dot(vp[pl.ds(pl.multiple_of(q * S, S), S), :], vp[...], 1, 1)
+    gterm[...] = dot(vp[pl.ds(pl.multiple_of(q * S, S), S), :], vp[...], 1, 1)
     get_a.wait()
     for h in range(2):
         c = q + h * NQ
@@ -179,47 +182,44 @@
                 cbuf[y, q] = pc[h, pl.ds(pl.multiple_of(q * S, S), S), :]
 
 
-    def sum_far(buf, got, s, r):
+    def sum_far(term, got, s, r):
         out = []
-        for k, (d, other) in enumerate(((8, 0), (8, 1), (FAR, 0), (-FAR, 0), (FAR, 1), (-FAR, 1), (0, 1))):
-            yy = 1 - y if other else y
-            out.append(copy_to(buf.at[0], got.at[k], s.at[k], r.at[k], yy * Z + plane(d), q))
+        for k, (d, yy) in enumerate(((FAR, y), (-FAR, y), (FAR, 1 - y), (-FAR, 1 - y), (0, 1 - y))):
+            out.append(copy_to(rows(term, yy, H), got.at[k], s.at[k], r.at[k], yy * Z + plane(d), q))
         return out
+
+    def sum_far_end(copies, term, buf, got):
+        for c in copies:
+            c.wait_recv()
+        above = got[1] + got[3]
+        buf[0] = (term[pl.ds(pl.multiple_of(y * H, H), H), :] + above) + (got[0] + got[2] + got[4])
+        buf[1] = above
 
     def sum_near(buf, got, s, r):
         return [
-            copy_to(buf.at[1], got.at[7 + k], s.at[7 + k], r.at[7 + k], y * Z + plane(d), q)
-            for k, d in enumerate((-2, 2, -1, 1))
+            copy_to(buf.at[1 if k == 0 else 0], got.at[5 + k], s.at[5 + k], r.at[5 + k], y * Z + plane(d), q)
+            for k, d in enumerate((-3, -2, 2, -1, 1))
         ]
 
-    def sum_far_end(copies, buf, got):
+    def sum_near_end(copies, buf, got):
         total = buf[0]
-        for k in range(2, 7):
-            copies[k].wait_recv()
-            total += got[k]
-        buf[1] = total
-
-    def sum_near_end(far, near, buf, got):
-        total = buf[1]
-        for k, c in enumerate(far[:2] + near):
+        for k, c in enumerate(copies):
             c.wait_recv()
-            total += got[k if k < 2 else k + 5]
+            total += got[5 + k]
         buf[2] = total
 
-    def all_copy(buf, dst, s, r, j):
-        return copy_to(buf.at[2], rows(dst, q), s.at[j], r.at[q], p, j)
-
     def all_send(buf, dst, s, r):
-        loop(1, NQ, lambda d: all_copy(buf, dst, s, r, lax.rem(q + d, NQ)).start())
-        dst[pl.ds(pl.multiple_of(q * S, S), S), :] = buf[2]
-
-    def all_wait(dst, s, r):
-        def one(j):
-            copy_to(rows(dst, j), rows(dst, j), s.at[0], r.at[j], p, q).wait_recv()
-
-        loop(0, NQ, lambda j: not_me(j, one))
-
-    g_far = sum_far(gs, gx, gx_s, gx_r)
+        def one(d):
+            i = lax.rem(y * NQ + q + d, 2 * NQ)
+            copy_to(buf.at[2], rows(dst, 2 * q + y, H), s.at[0], r.at[0], i // NQ * Z + z, lax.rem(i, NQ)).start()
+
+        loop(1, 2 * NQ, one)
+        dst[pl.ds(pl.multiple_of((2 * q + y) * H, H), H), :] = buf[2]
+
+    def all_rows(dst, s, r):
+        return copy_to(dst.at[pl.ds(0, T - H)], dst.at[pl.ds(0, T - H)], s.at[0], r.at[0], p, mate)
+
+    g_far = sum_far(gterm, gx, gx_s, gx_r)
     for c in g_far:
         c.start()
 
@@ -289,7 +289,7 @@
         loop(0, n, add)
 
 
-    sum_far_end(g_far, gs, gx)
+    sum_far_end(g_far, gterm, gs, gx)
     g_near = sum_near(gs, gx, gx_s, gx_r)
     for c in g_near:
         c.start()
@@ -319,7 +319,7 @@
         c3_sum(k)
         c3_copy(k).start()
 
-    sum_near_end(g_far, g_near, gs, gx)
+    sum_near_end(g_near, gs, gx)
     all_send(gs, gram, ga_s, ga_r)
     c3_sum(0)
 
@@ -333,8 +333,8 @@
         wsl[...] += rowbuf[j]
 
     loop(0, last_q + 1, row_add)
-    ms[0] = dot(wsl[...], vp[...], 1, 1)
-    m_far = sum_far(ms, mx, mx_s, mx_r)
+    mterm[...] = dot(wsl[...], vp[...], 1, 1)
+    m_far = sum_far(mterm, mx, mx_s, mx_r)
     for c in m_far:
         c.start()
 
@@ -347,12 +347,35 @@
     fan(0, wsl, w_dst, w_s, w_r)
 
     def wrow_copy(j):
-        return copy_to(wsl, rows(wp, q), wr_s.at[j], wr_r.at[q], p, j)
+        return copy_to(wsl, rows(wp, q), wr_s.at[j], wr_r.at[0], p, j)
 
     loop(0, last_q + 1, lambda j: not_me(j, lambda i: wrow_copy(i).start()))
     wp[pl.ds(pl.multiple_of(q * S, S), S), :] = wsl[...]
 
-    all_wait(gram, ga_s, ga_r)
+    for k, src in enumerate((v_mine, vrel.at[0], vrel.at[1])):
+        fan_done(k, src, v_dst, v_s, v_r)
+    for h in range(2):
+        @pl.when(q + h * NQ <= p)
+        def _():
+            c1_each(h, lambda c: c.wait_send())
+
+    def c2_sent(n, i, b):
+        @pl.when(b != 0)
+        def _():
+            c2_copy(n).wait_send()
+
+    c2_each(c2_sent)
+    for k in (1, 2):
+        c3_copy(k).wait_send()
+
+    @pl.when(q <= p)
+    def _():
+        loop(1, NQ, lambda d: row_copy(lax.rem(q + d, NQ)).wait_send())
+
+    for c in v_first + g_far + g_near:
+        c.wait_send()
+
+    all_rows(gram, ga_s, ga_r).wait_recv()
     diag = jnp.where(ii == jj, 0.5 * gram[...], 0.0)
     power = jnp.where(ii < jj, -gram[...], 0.0) / jnp.sum(diag, axis=1, keepdims=True)
     stack[0:T] = jnp.where(ii == jj, 1.0, power)
@@ -365,7 +388,7 @@
 
     loop(0, 4, double)
 
-    sum_far_end(m_far, ms, mx)
+    sum_far_end(m_far, mterm, ms, mx)
     m_near = sum_near(ms, mx, mx_s, mx_r)
     for c in m_near:
         c.start()
@@ -376,7 +399,7 @@
     loop(0, 2, double)
     coef[...] = (stack[0:T] + dot(stack[0:T], stack[T:])) / jnp.sum(diag, axis=0, keepdims=True)
 
-    sum_near_end(m_far, m_near, ms, mx)
+    sum_near_end(m_near, ms, mx)
     all_send(ms, mtot, ma_s, ma_r)
     yp[...] = dot(coef[...], vp[...])
     lhs[T:] = -yp[...]
@@ -387,10 +410,8 @@
 
     @pl.when(q <= p)
     def _():
-        def wr_wait(j):
-            copy_to(rows(wp, j), rows(wp, j), wr_s.at[0], wr_r.at[j], p, q).wait_recv()
-
-        loop(0, NQ, lambda j: not_me(j, wr_wait))
+        others = wp.at[pl.ds(0, T - S)]
+        copy_to(others, others, wr_s.at[0], wr_r.at[0], p, mate).wait_recv()
         lhs[0:T] = -wp[...]
 
     for h in range(2):
@@ -410,7 +431,14 @@
             sym = jnp.where(c < p, tile, 0.5 * (tile + tile.T))
             low[h] = sym + dot(lhs[...], rhs[h], 0, 0)
 
-    all_wait(mtot, ma_s, ma_r)
+    for k, src in enumerate((wsl, wrel.at[0], wrel.at[1])):
+        fan_done(k, src, w_dst, w_s, w_r)
+    loop(0, last_q + 1, lambda j: not_me(j, lambda i: wrow_copy(i).wait_send()))
+    all_rows(gram, ga_s, ga_r).wait_send()
+    for c in w_first + m_far + m_near:
+        c.wait_send()
+
+    all_rows(mtot, ma_s, ma_r).wait_recv()
     wp[...] = dot(mtot[...] + mtot[...].T, yp[...])
     for h in range(2):
         c = q + h * NQ
@@ -423,32 +451,7 @@
         def _():
             o_ref[:, h, :] = jnp.zeros((T, T), f32)
 
-    for k, (v_src, w_src) in enumerate(((v_mine, wsl), (vrel.at[0], wrel.at[0]), (vrel.at[1], wrel.at[1]))):
-        fan_done(k, v_src, v_dst, v_s, v_r)
-        fan_done(k, w_src, w_dst, w_s, w_r)
-    for h in range(2):
-        @pl.when(q + h * NQ <= p)
-        def _():
-            c1_each(h, lambda c: c.wait_send())
-
-    def c2_sent(n, i, b):
-        @pl.when(b != 0)
-        def _():
-            c2_copy(n).wait_send()
-
-    c2_each(c2_sent)
-    for k in (1, 2):
-        c3_copy(k).wait_send()
-
-    @pl.when(q <= p)
-    def _():
-        loop(1, NQ, lambda d: row_copy(lax.rem(q + d, NQ)).wait_send())
-
-    loop(0, last_q + 1, lambda j: not_me(j, lambda i: wrow_copy(i).wait_send()))
-    loop(1, NQ, lambda d: all_copy(gs, gram, ga_s, ga_r, lax.rem(q + d, NQ)).wait_send())
-    loop(1, NQ, lambda d: all_copy(ms, mtot, ma_s, ma_r, lax.rem(q + d, NQ)).wait_send())
-    for c in v_first + w_first + g_far + g_near + m_far + m_near:
-        c.wait_send()
+    all_rows(mtot, ma_s, ma_r).wait_send()
 
 
 def body(matrix, reflectors):
@@ -464,13 +467,14 @@
             vmem(T, T), vmem(2, T, T), vmem(2, T, T), vmem(2, T, T),
             vmem(2, NQ, S, T), vmem(3, 6, S, T), vmem(3, S, T), vmem(2, S, T), vmem(NQ, S, T),
             vmem(T, T), vmem(S, T), vmem(T, T), vmem(2, S, T), vmem(2, S, T),
-            vmem(3, S, T), vmem(11, S, T), vmem(T, T), vmem(3, S, T), vmem(11, S, T), vmem(T, T),
+            vmem(S, T), vmem(3, H, T), vmem(10, H, T), vmem(T, T),
+            vmem(S, T), vmem(3, H, T), vmem(10, H, T), vmem(T, T),
             vmem(2 * T, T), vmem(T, T), vmem(T, T), vmem(2 * T, T), vmem(2, 2 * T, T),
             dma(2), dma(3, 12), dma(2), dma(2), dma(2), dma(3, 12), dma(2), dma(2), dma(2),
-            dma(2, NQ), dma(2, NQ), dma(Z), dma(3, 6), dma(2), dma(2), dma(NQ), dma(NQ), dma(NQ), dma(NQ),
-            dma(11), dma(11), dma(NQ), dma(NQ), dma(11), dma(11), dma(NQ), dma(NQ),
+            dma(2, NQ), dma(2, NQ), dma(Z), dma(3, 6), dma(2), dma(2), dma(NQ), dma(NQ), dma(NQ), dma(1),
+            dma(10), dma(10), dma(1), dma(1), dma(10), dma(10), dma(1), dma(1),
         ],
-        compiler_params=pltpu.CompilerParams(collective_id=0, has_side_effects=True, vmem_limit_bytes=60 * 2**20),
+        compiler_params=pltpu.CompilerParams(collective_id=0, has_side_effects=True, vmem_limit_bytes=53 * 2**20),
         cost_estimate=pl.CostEstimate(flops=34 * 2 * T**3, bytes_accessed=5 * T * T * 4, transcendentals=0),
     )(matrix.reshape(T, 2, T), reflectors.reshape(T, T))
     return out.reshape(matrix.shape)

time: 76 us -> 64.3 us (0.85)
  Pallas kernels: 73.8 us -> 62.3 us
    pallas_call x1, Pallas kernels: 73.8 us -> 62.3 us  [body(): pl.pallas_call(kernel, out_shape=jax.ShapeDtypeStruct((T, 2, T), f32), in...]
    unnamed x1 -> x3, local copies, waits for them, and re-layouts: 2.01 us -> 1.75 us
where the time goes in v6:
time: 64.3 us; the launch traced here: 64.1 us
  Pallas kernels  62.3 us (97%)
  local copies, waits for them, and re-layouts  1.75 us (3%)
    pallas_call x1, Pallas kernels, body(): pl.pallas_call(kernel, out_shape=jax.ShapeDtypeStruct((T, 2, T), f32), in...  62.3 us
    unnamed x3, local copies, waits for them, and re-layouts  1.75 us

profile of v6, /device:TPU:1, one launch (start us, length us, event | category | flops | bytes accessed | tf_op | source)
XLA Modules:
  0.0 64.1 jit_solution(9173824552917289437)
XLA Ops:
  0.0 0.0 copy-start
  0.0 0.9 %copy-done = f32[1,256,256]{2,1,0:T(8,128)S(1)} copy-done((f32[1,256,256]{2,1,0:T(8,128)S(1)}, f32[1,256,256]{2,1,0:T(8,128)}, u32[]{:S(2)}) %copy-start) | copy-done | bytes 262168
  1.0 62.3 %shard_map.28 = f32[256,2,256]{2,1,0:T(2,128)S(1)} custom-call(f32[256,2,256]{2,1,0:T(2,128)} %bitcast.5, f32[256,256]{1,0:T(8,128)S(1)} %bitcast.4), custom_call_target="tpu_custom_call" | custom-call | flops 1140850688 | bytes 1310720 | tf_op jit(solution)/shard_map/pallas_call | solution.py:460
  63.3 0.8 %copy.4 = f32[1,256,2,256]{3,2,1,0:T(2,128)} copy(f32[1,256,2,256]{3,2,1,0:T(2,128)S(1)} %bitcast.3) | data formatting | bytes 1048576
Async XLA Ops:
  0.0 0.9 %copy-start = (f32[1,256,256]{2,1,0:T(8,128)S(1)}, f32[1,256,256]{2,1,0:T(8,128)}, u32[]{:S(2)}) copy-start(f32[1,256,256]{2,1,0:T(8,128)} %param.3) | copy-start | bytes 786436

commit v7 on v6

--- a/solution.py
+++ b/solution.py
@@ -53,6 +53,25 @@
     def plane(d):
         return lax.rem(z + d + Z, Z)
 
+    def some(n):
+        ref = stack.at[pl.ds(0, n)]
+        return ref, ref
+
+    def sent(n, sem):
+        copy_to(*some(n), sem, sem, p, mate).wait_send()
+
+    def got(n, sem):
+        copy_to(*some(n), sem, sem, p, mate).wait_recv()
+
+    def if_any(n, fn, sem, most, least=0):
+        if most == least:
+            if most:
+                fn(most * S, sem)
+            return
+        half = (least + most) // 2
+        pl.when(n <= half)(lambda: if_any(n, fn, sem, half, least))
+        pl.when(n > half)(lambda: if_any(n, fn, sem, most, half + 1))
+
     def not_me(j, fn):
         @pl.when(j != q)
         def _():
@@ -95,12 +114,12 @@
 
     loop(1, NQ, lambda d: greet(p, lax.rem(q + d, NQ)))
     loop(0, NQ, lambda j: greet((1 - y) * Z + z, j))
-    count = jnp.int32(9 + 31)
+    fans = jnp.int32(0)
     for k in range(3):
         t, n = source(k)
         for i in range(2 * n):
             pp = (i % 2) * Z + plane(i // 2 - 2)
-            count += ((pp > y * Z + t) & ((pp != p) | (t != q))).astype(jnp.int32)
+            fans += ((pp > y * Z + t) & ((pp != p) | (t != q))).astype(jnp.int32)
 
     get_r.wait()
     raw = r_ref[...]
@@ -123,33 +142,25 @@
         def _():
             vc[h] = vp[...]
 
-    pl.semaphore_wait(barrier, count)
+    pl.semaphore_wait(barrier, 9 + 31 + fans)
 
     def first(src, rel, f_s, f_r):
         return [
-            copy_to(src, rel.at[0], f_s.at[0], f_r.at[0], y * Z + plane(FAR), q),
-            copy_to(src, rel.at[1], f_s.at[1], f_r.at[1], y * Z + plane(-FAR), q),
+            copy_to(src, rel.at[0], f_s, f_r.at[0], y * Z + plane(FAR), q),
+            copy_to(src, rel.at[1], f_s, f_r.at[1], y * Z + plane(-FAR), q),
         ]
 
     def fan(k, src, dst, s_s, s_r):
         def send(i, pp, t, live, me):
             @pl.when(live & jnp.logical_not(me))
             def _():
-                copy_to(src, dst, s_s.at[k, i], s_r.at[y], pp, t).start()
+                copy_to(src, dst, s_s, s_r.at[y], pp, t).start()
 
             @pl.when(live & me)
             def _():
                 pltpu.make_async_copy(src, dst, s_r.at[y]).start()
 
         targets(k, send)
-
-    def fan_done(k, src, dst, s_s, s_r):
-        def done(i, pp, t, live, me):
-            @pl.when(live & jnp.logical_not(me))
-            def _():
-                copy_to(src, dst, s_s.at[k, i], s_r.at[y], pp, t).wait_send()
-
-        targets(k, done)
 
     v_mine = rows(vp, q)
     v_dst = rows(vc.at[y], q)
@@ -160,7 +171,7 @@
     fan(0, v_mine, v_dst, v_s, v_r)
 
     def c1_copy(h, j):
-        return copy_to(rows(pc.at[h], j), cbuf.at[y, q], c1_s.at[h, j], c1_r.at[y, q], h * Z + z, j)
+        return copy_to(rows(pc.at[h], j), cbuf.at[y, q], c1_s.at[h], c1_r.at[y], h * Z + z, j)
 
     def c1_each(h, fn):
         def one(d):
@@ -182,58 +193,49 @@
                 cbuf[y, q] = pc[h, pl.ds(pl.multiple_of(q * S, S), S), :]
 
 
-    def sum_far(term, got, s, r):
+    def sum_far(term, parts, s, r):
         out = []
         for k, (d, yy) in enumerate(((FAR, y), (-FAR, y), (FAR, 1 - y), (-FAR, 1 - y), (0, 1 - y))):
-            out.append(copy_to(rows(term, yy, H), got.at[k], s.at[k], r.at[k], yy * Z + plane(d), q))
+            out.append(copy_to(rows(term, yy, H), parts.at[k], s, r.at[0], yy * Z + plane(d), q))
         return out
 
-    def sum_far_end(copies, term, buf, got):
-        for c in copies:
-            c.wait_recv()
-        above = got[1] + got[3]
-        buf[0] = (term[pl.ds(pl.multiple_of(y * H, H), H), :] + above) + (got[0] + got[2] + got[4])
+    def sum_far_end(term, buf, parts, r):
+        got(5 * H, r.at[0])
+        above = parts[1] + parts[3]
+        buf[0] = (term[pl.ds(pl.multiple_of(y * H, H), H), :] + above) + (parts[0] + parts[2] + parts[4])
         buf[1] = above
 
-    def sum_near(buf, got, s, r):
+    def sum_near(buf, parts, s, r):
         return [
-            copy_to(buf.at[1 if k == 0 else 0], got.at[5 + k], s.at[5 + k], r.at[5 + k], y * Z + plane(d), q)
+            copy_to(buf.at[1 if k == 0 else 0], parts.at[5 + k], s, r.at[1], y * Z + plane(d), q)
             for k, d in enumerate((-3, -2, 2, -1, 1))
         ]
 
-    def sum_near_end(copies, buf, got):
+    def sum_near_end(buf, parts, r):
+        got(5 * H, r.at[1])
         total = buf[0]
-        for k, c in enumerate(copies):
-            c.wait_recv()
-            total += got[5 + k]
+        for k in range(5):
+            total += parts[5 + k]
         buf[2] = total
 
     def all_send(buf, dst, s, r):
         def one(d):
             i = lax.rem(y * NQ + q + d, 2 * NQ)
-            copy_to(buf.at[2], rows(dst, 2 * q + y, H), s.at[0], r.at[0], i // NQ * Z + z, lax.rem(i, NQ)).start()
+            copy_to(buf.at[2], rows(dst, 2 * q + y, H), s, r, i // NQ * Z + z, lax.rem(i, NQ)).start()
 
         loop(1, 2 * NQ, one)
         dst[pl.ds(pl.multiple_of((2 * q + y) * H, H), H), :] = buf[2]
 
-    def all_rows(dst, s, r):
-        return copy_to(dst.at[pl.ds(0, T - H)], dst.at[pl.ds(0, T - H)], s.at[0], r.at[0], p, mate)
-
     g_far = sum_far(gterm, gx, gx_s, gx_r)
     for c in g_far:
         c.start()
 
     def relay(k, rel, f_s, f_r, dst, s_s, s_r):
-        copy_to(rel.at[k - 1], rel.at[k - 1], f_s.at[k - 1], f_r.at[k - 1], p, q).wait_recv()
+        copy_to(rel.at[k - 1], rel.at[k - 1], f_s, f_r.at[k - 1], p, q).wait_recv()
         fan(k, rel.at[k - 1], dst, s_s, s_r)
 
     for k in (1, 2):
         relay(k, vrel, vf_s, vf_r, v_dst, v_s, v_r)
-
-    def c1_wait(yy, i):
-        @pl.when((yy != y) | (i != q))
-        def _():
-            copy_to(cbuf.at[yy, i], cbuf.at[yy, i], c1_s.at[0, 0], c1_r.at[yy, i], p, q).wait_recv()
 
     def group(n):
         off = jnp.where(n < 6, n + 3, jnp.where(n < 11, 3 - n, n - 13))
@@ -243,7 +245,7 @@
 
     def c2_copy(n):
         i, k, a, b = group(n)
-        return copy_to(cbuf.at[1, i], nbuf.at[k, b + 2], c2_s.at[n], c2_r.at[k, b + 2], y * Z + plane(-b), q)
+        return copy_to(cbuf.at[1, i], nbuf.at[k, b + 2], c2_s, c2_r.at[k], y * Z + plane(-b), q)
 
     def c2_each(fn):
         def one(n):
@@ -256,21 +258,25 @@
         loop(0, Z, one)
 
     def c2_send(n, i, b):
-        c1_wait(1, i)
-
         @pl.when((y == 0) & (i <= z))
         def _():
-            c1_wait(0, i)
             cbuf[1, i] += cbuf[0, i]
 
         @pl.when(b != 0)
         def _():
             c2_copy(n).start()
 
+    own = (q <= z).astype(jnp.int32)
+    if_any(z + 1 - own, got, c1_r.at[y], NQ)
+
+    @pl.when(y == 0)
+    def _():
+        got(T, c1_r.at[1])
+
     c2_each(c2_send)
 
     def c3_copy(k):
-        return copy_to(psum.at[k], abuf.at[k - 1], c3_s.at[k - 1], c3_r.at[k - 1], y * Z + source(k)[0], q)
+        return copy_to(psum.at[k], abuf.at[k - 1], c3_s, c3_r, y * Z + source(k)[0], q)
 
     def c3_sum(k):
         t, n = source(k)
@@ -280,16 +286,18 @@
         def _():
             psum[k] = cbuf[1, t]
 
+        live = [((y == 0) | (t <= plane(i - 2))).astype(jnp.int32) for i in range(n) if i != 2]
+        if_any(sum(live), got, c2_r.at[k], n - 1)
+
         def add(i):
             @pl.when((i != 2) & ((y == 0) | (t <= plane(i - 2))))
             def _():
-                copy_to(nbuf.at[k, i], nbuf.at[k, i], c2_s.at[0], c2_r.at[k, i], p, q).wait_recv()
                 psum[k] += nbuf[k, i]
 
         loop(0, n, add)
 
 
-    sum_far_end(g_far, gterm, gs, gx)
+    sum_far_end(gterm, gs, gx, gx_r)
     g_near = sum_near(gs, gx, gx_s, gx_r)
     for c in g_near:
         c.start()
@@ -297,7 +305,7 @@
     for h in range(2):
         @pl.when(q + h * NQ < p)
         def _():
-            copy_to(vc.at[h], vc.at[h], v_s.at[0, 0], v_r.at[h], p, q).wait_recv()
+            copy_to(vc.at[h], vc.at[h], v_s, v_r.at[h], p, q).wait_recv()
 
     @pl.when(q <= p)
     def _():
@@ -308,7 +316,7 @@
         rpart[...] += dot(vc[1], low[1], 1, 1)
 
     def row_copy(j):
-        return copy_to(rows(rpart, j), rowbuf.at[q], row_s.at[j], row_r.at[q], p, j)
+        return copy_to(rows(rpart, j), rowbuf.at[q], row_s, row_r, p, j)
 
     @pl.when(q <= p)
     def _():
@@ -319,17 +327,16 @@
         c3_sum(k)
         c3_copy(k).start()
 
-    sum_near_end(g_near, gs, gx)
+    sum_near_end(gs, gx, gx_r)
     all_send(gs, gram, ga_s, ga_r)
     c3_sum(0)
 
     wsl[...] = jnp.zeros((S, T), f32)
 
+    others = last_q + 1 - (q <= last_q).astype(jnp.int32)
+    if_any(others, got, row_r, NQ)
+
     def row_add(j):
-        @pl.when(j != q)
-        def _():
-            copy_to(rowbuf.at[j], rowbuf.at[j], row_s.at[0], row_r.at[j], p, q).wait_recv()
-
         wsl[...] += rowbuf[j]
 
     loop(0, last_q + 1, row_add)
@@ -338,8 +345,7 @@
     for c in m_far:
         c.start()
 
-    for k in (1, 2):
-        copy_to(abuf.at[k - 1], abuf.at[k - 1], c3_s.at[0], c3_r.at[k - 1], p, q).wait_recv()
+    got(2 * S, c3_r)
     wsl[...] += (psum[0] + abuf[0]) + abuf[1]
     w_first = first(wsl, wrel, wf_s, wf_r)
     for c in w_first:
@@ -347,35 +353,35 @@
     fan(0, wsl, w_dst, w_s, w_r)
 
     def wrow_copy(j):
-        return copy_to(wsl, rows(wp, q), wr_s.at[j], wr_r.at[0], p, j)
+        return copy_to(wsl, rows(wp, q), wr_s, wr_r, p, j)
 
     loop(0, last_q + 1, lambda j: not_me(j, lambda i: wrow_copy(i).start()))
     wp[pl.ds(pl.multiple_of(q * S, S), S), :] = wsl[...]
 
-    for k, src in enumerate((v_mine, vrel.at[0], vrel.at[1])):
-        fan_done(k, src, v_dst, v_s, v_r)
-    for h in range(2):
-        @pl.when(q + h * NQ <= p)
-        def _():
-            c1_each(h, lambda c: c.wait_send())
-
-    def c2_sent(n, i, b):
-        @pl.when(b != 0)
-        def _():
-            c2_copy(n).wait_send()
-
-    c2_each(c2_sent)
-    for k in (1, 2):
-        c3_copy(k).wait_send()
+    if_any(fans, sent, v_s, 32)
+    sent(2 * S, vf_s)
+    for h in range(2):
+        @pl.when((q + h * NQ <= p) & (h == y))
+        def _():
+            sent(T - S, c1_s.at[h])
+
+        @pl.when((q + h * NQ <= p) & (h != y))
+        def _():
+            sent(T, c1_s.at[h])
+
+    live = jnp.where(y == 0, Z, z + 1)
+    for k in range(3):
+        live -= ((y == 0) | (source(k)[0] <= z)).astype(jnp.int32)
+    if_any(live, sent, c2_s, Z)
+    sent(2 * S, c3_s)
 
     @pl.when(q <= p)
     def _():
-        loop(1, NQ, lambda d: row_copy(lax.rem(q + d, NQ)).wait_send())
-
-    for c in v_first + g_far + g_near:
-        c.wait_send()
-
-    all_rows(gram, ga_s, ga_r).wait_recv()
+        sent(T - S, row_s)
+
+    sent(10 * H, gx_s)
+
+    got(T - H, ga_r)
     diag = jnp.where(ii == jj, 0.5 * gram[...], 0.0)
     power = jnp.where(ii < jj, -gram[...], 0.0) / jnp.sum(diag, axis=1, keepdims=True)
     stack[0:T] = jnp.where(ii == jj, 1.0, power)
@@ -388,7 +394,7 @@
 
     loop(0, 4, double)
 
-    sum_far_end(m_far, mterm, ms, mx)
+    sum_far_end(mterm, ms, mx, mx_r)
     m_near = sum_near(ms, mx, mx_s, mx_r)
     for c in m_near:
         c.start()
@@ -399,7 +405,7 @@
     loop(0, 2, double)
     coef[...] = (stack[0:T] + dot(stack[0:T], stack[T:])) / jnp.sum(diag, axis=0, keepdims=True)
 
-    sum_near_end(m_near, ms, mx)
+    sum_near_end(ms, mx, mx_r)
     all_send(ms, mtot, ma_s, ma_r)
     yp[...] = dot(coef[...], vp[...])
     lhs[T:] = -yp[...]
@@ -410,8 +416,7 @@
 
     @pl.when(q <= p)
     def _():
-        others = wp.at[pl.ds(0, T - S)]
-        copy_to(others, others, wr_s.at[0], wr_r.at[0], p, mate).wait_recv()
+        got(T - S, wr_r)
         lhs[0:T] = -wp[...]
 
     for h in range(2):
@@ -419,7 +424,7 @@
 
         @pl.when(c < p)
         def _():
-            copy_to(rhs.at[h, pl.ds(T, T)], rhs.at[h, pl.ds(T, T)], w_s.at[0, 0], w_r.at[h], p, q).wait_recv()
+            copy_to(rhs.at[h, pl.ds(T, T)], rhs.at[h, pl.ds(T, T)], w_s, w_r.at[h], p, q).wait_recv()
 
         @pl.when(c == p)
         def _():
@@ -431,14 +436,13 @@
             sym = jnp.where(c < p, tile, 0.5 * (tile + tile.T))
             low[h] = sym + dot(lhs[...], rhs[h], 0, 0)
 
-    for k, src in enumerate((wsl, wrel.at[0], wrel.at[1])):
-        fan_done(k, src, w_dst, w_s, w_r)
-    loop(0, last_q + 1, lambda j: not_me(j, lambda i: wrow_copy(i).wait_send()))
-    all_rows(gram, ga_s, ga_r).wait_send()
-    for c in w_first + m_far + m_near:
-        c.wait_send()
-
-    all_rows(mtot, ma_s, ma_r).wait_recv()
+    if_any(fans, sent, w_s, 32)
+    sent(2 * S, wf_s)
+    if_any(others, sent, wr_s, NQ)
+    sent(T - H, ga_s)
+    sent(10 * H, mx_s)
+
+    got(T - H, ma_r)
     wp[...] = dot(mtot[...] + mtot[...].T, yp[...])
     for h in range(2):
         c = q + h * NQ
@@ -451,12 +455,13 @@
         def _():
             o_ref[:, h, :] = jnp.zeros((T, T), f32)
 
-    all_rows(mtot, ma_s, ma_r).wait_send()
+    sent(T - H, ma_s)
 
 
 def body(matrix, reflectors):
     vmem = lambda *shape: pltpu.VMEM(shape, f32)
     dma = lambda *shape: pltpu.SemaphoreType.DMA(shape)
+    one = pltpu.SemaphoreType.DMA
     out = pl.pallas_call(
         kernel,
         out_shape=jax.ShapeDtypeStruct((T, 2, T), f32),
@@ -470,9 +475,9 @@
             vmem(S, T), vmem(3, H, T), vmem(10, H, T), vmem(T, T),
             vmem(S, T), vmem(3, H, T), vmem(10, H, T), vmem(T, T),
             vmem(2 * T, T), vmem(T, T), vmem(T, T), vmem(2 * T, T), vmem(2, 2 * T, T),
-            dma(2), dma(3, 12), dma(2), dma(2), dma(2), dma(3, 12), dma(2), dma(2), dma(2),
-            dma(2, NQ), dma(2, NQ), dma(Z), dma(3, 6), dma(2), dma(2), dma(NQ), dma(NQ), dma(NQ), dma(1),
-            dma(10), dma(10), dma(1), dma(1), dma(10), dma(10), dma(1), dma(1),
+            dma(2), one, dma(2), one, dma(2), one, dma(2), one, dma(2),
+            dma(2), dma(2), one, dma(3), one, one, one, one, one, one,
+            one, dma(2), one, one, one, dma(2), one, one,
         ],
         compiler_params=pltpu.CompilerParams(collective_id=0, has_side_effects=True, vmem_limit_bytes=53 * 2**20),
         cost_estimate=pl.CostEstimate(flops=34 * 2 * T**3, bytes_accessed=5 * T * T * 4, transcendentals=0),

time: 64.3 us -> 61.6 us (0.958)
  Pallas kernels: 62.3 us -> 59.7 us
    pallas_call x1, Pallas kernels: 62.3 us -> 59.7 us  [body(): pl.pallas_call(kernel, out_shape=jax.ShapeDtypeStruct((T, 2, T), f32), in...]
where the time goes in v7:
time: 61.6 us; the launch traced here: 61.5 us
  Pallas kernels  59.7 us (97%)
  local copies, waits for them, and re-layouts  1.75 us (3%)
    pallas_call x1, Pallas kernels, body(): pl.pallas_call(kernel, out_shape=jax.ShapeDtypeStruct((T, 2, T), f32), in...  59.7 us
    unnamed x3, local copies, waits for them, and re-layouts  1.75 us

profile of v7, /device:TPU:1, one launch (start us, length us, event | category | flops | bytes accessed | tf_op | source)
XLA Modules:
  0.0 61.5 jit_solution(928322967301730757)
XLA Ops:
  0.0 0.0 copy-start
  0.0 0.9 %copy-done = f32[1,256,256]{2,1,0:T(8,128)S(1)} copy-done((f32[1,256,256]{2,1,0:T(8,128)S(1)}, f32[1,256,256]{2,1,0:T(8,128)}, u32[]{:S(2)}) %copy-start) | copy-done | bytes 262168
  1.0 59.7 %shard_map.28 = f32[256,2,256]{2,1,0:T(2,128)S(1)} custom-call(f32[256,2,256]{2,1,0:T(2,128)} %bitcast.5, f32[256,256]{1,0:T(8,128)S(1)} %bitcast.4), custom_call_target="tpu_custom_call" | custom-call | flops 1140850688 | bytes 1310720 | tf_op jit(solution)/shard_map/pallas_call | solution.py:465
  60.7 0.8 %copy.4 = f32[1,256,2,256]{3,2,1,0:T(2,128)} copy(f32[1,256,2,256]{3,2,1,0:T(2,128)S(1)} %bitcast.3) | data formatting | bytes 1048576
Async XLA Ops:
  0.0 0.9 %copy-start = (f32[1,256,256]{2,1,0:T(8,128)S(1)}, f32[1,256,256]{2,1,0:T(8,128)}, u32[]{:S(2)}) copy-start(f32[1,256,256]{2,1,0:T(8,128)} %param.3) | copy-start | bytes 786436

commit v8 on v7

--- a/solution.py
+++ b/solution.py
@@ -127,20 +127,6 @@
     jj = lax.broadcasted_iota(jnp.int32, (T, T), 1)
     unit = jnp.where(ii > jj, raw, jnp.where(ii == jj, 1.0, 0.0))
     vp[...] = jnp.where(p == 0, 0.0, jnp.where(p == 1, unit, raw)).T
-    gterm[...] = dot(vp[pl.ds(pl.multiple_of(q * S, S), S), :], vp[...], 1, 1)
-    get_a.wait()
-    for h in range(2):
-        c = q + h * NQ
-
-        @pl.when(c <= p)
-        def _():
-            tile = a_ref[:, h, :] * jnp.where(c < p, 1.0, 0.5)
-            low[h] = tile
-            pc[h] = dot(vp[...], tile)
-
-        @pl.when(c == p)
-        def _():
-            vc[h] = vp[...]
 
     pl.semaphore_wait(barrier, 9 + 31 + fans)
 
@@ -169,6 +155,21 @@
     for c in v_first:
         c.start()
     fan(0, v_mine, v_dst, v_s, v_r)
+
+    gterm[...] = dot(vp[pl.ds(pl.multiple_of(q * S, S), S), :], vp[...], 1, 1)
+    get_a.wait()
+    for h in range(2):
+        c = q + h * NQ
+
+        @pl.when(c <= p)
+        def _():
+            tile = a_ref[:, h, :] * jnp.where(c < p, 1.0, 0.5)
+            low[h] = tile
+            pc[h] = dot(vp[...], tile)
+
+        @pl.when(c == p)
+        def _():
+            vc[h] = vp[...]
 
     def c1_copy(h, j):
         return copy_to(rows(pc.at[h], j), cbuf.at[y, q], c1_s.at[h], c1_r.at[y], h * Z + z, j)

time: 61.6 us -> 61.1 us (level)
  no operation moved by 1% of the time
where the time goes in v8:
time: 61.1 us; the launch traced here: 61 us
  Pallas kernels  59.3 us (97%)
  local copies, waits for them, and re-layouts  1.75 us (3%)
    pallas_call x1, Pallas kernels, body(): pl.pallas_call(kernel, out_shape=jax.ShapeDtypeStruct((T, 2, T), f32), in...  59.3 us
    unnamed x3, local copies, waits for them, and re-layouts  1.75 us

profile of v8, /device:TPU:1, one launch (start us, length us, event | category | flops | bytes accessed | tf_op | source)
XLA Modules:
  0.0 61.0 jit_solution(16329184441205181592)
XLA Ops:
  0.0 0.0 copy-start
  0.0 0.9 %copy-done = f32[1,256,256]{2,1,0:T(8,128)S(1)} copy-done((f32[1,256,256]{2,1,0:T(8,128)S(1)}, f32[1,256,256]{2,1,0:T(8,128)}, u32[]{:S(2)}) %copy-start) | copy-done | bytes 262168
  1.0 59.3 %shard_map.28 = f32[256,2,256]{2,1,0:T(2,128)S(1)} custom-call(f32[256,2,256]{2,1,0:T(2,128)} %bitcast.5, f32[256,256]{1,0:T(8,128)S(1)} %bitcast.4), custom_call_target="tpu_custom_call" | custom-call | flops 1140850688 | bytes 1310720 | tf_op jit(solution)/shard_map/pallas_call | solution.py:466
  60.2 0.8 %copy.4 = f32[1,256,2,256]{3,2,1,0:T(2,128)} copy(f32[1,256,2,256]{3,2,1,0:T(2,128)S(1)} %bitcast.3) | data formatting | bytes 1048576
Async XLA Ops:
  0.0 0.9 %copy-start = (f32[1,256,256]{2,1,0:T(8,128)S(1)}, f32[1,256,256]{2,1,0:T(8,128)}, u32[]{:S(2)}) copy-start(f32[1,256,256]{2,1,0:T(8,128)} %param.3) | copy-start | bytes 786436

commit v9 on v8

--- a/solution.py
+++ b/solution.py
@@ -224,7 +224,8 @@
             i = lax.rem(y * NQ + q + d, 2 * NQ)
             copy_to(buf.at[2], rows(dst, 2 * q + y, H), s, r, i // NQ * Z + z, lax.rem(i, NQ)).start()
 
-        loop(1, 2 * NQ, one)
+        for d in range(1, 2 * NQ):
+            one(d)
         dst[pl.ds(pl.multiple_of((2 * q + y) * H, H), H), :] = buf[2]
 
     g_far = sum_far(gterm, gx, gx_s, gx_r)

time: 61.1 us -> 61.5 us (level)
  no operation moved by 1% of the time
where the time goes in v9:
time: 61.5 us; the launch traced here: 61.4 us
  Pallas kernels  59.6 us (97%)
  local copies, waits for them, and re-layouts  1.75 us (3%)
    pallas_call x1, Pallas kernels, body(): pl.pallas_call(kernel, out_shape=jax.ShapeDtypeStruct((T, 2, T), f32), in...  59.6 us
    unnamed x3, local copies, waits for them, and re-layouts  1.75 us

profile of v9, /device:TPU:1, one launch (start us, length us, event | category | flops | bytes accessed | tf_op | source)
XLA Modules:
  0.0 61.4 jit_solution(13269026266626886201)
XLA Ops:
  0.0 0.0 copy-start
  0.0 0.9 %copy-done = f32[1,256,256]{2,1,0:T(8,128)S(1)} copy-done((f32[1,256,256]{2,1,0:T(8,128)S(1)}, f32[1,256,256]{2,1,0:T(8,128)}, u32[]{:S(2)}) %copy-start) | copy-done | bytes 262168
  1.0 59.6 %shard_map.28 = f32[256,2,256]{2,1,0:T(2,128)S(1)} custom-call(f32[256,2,256]{2,1,0:T(2,128)} %bitcast.5, f32[256,256]{1,0:T(8,128)S(1)} %bitcast.4), custom_call_target="tpu_custom_call" | custom-call | flops 1140850688 | bytes 1310720 | tf_op jit(solution)/shard_map/pallas_call | solution.py:467
  60.6 0.8 %copy.4 = f32[1,256,2,256]{3,2,1,0:T(2,128)} copy(f32[1,256,2,256]{3,2,1,0:T(2,128)S(1)} %bitcast.3) | data formatting | bytes 1048576
Async XLA Ops:
  0.0 0.9 %copy-start = (f32[1,256,256]{2,1,0:T(8,128)S(1)}, f32[1,256,256]{2,1,0:T(8,128)}, u32[]{:S(2)}) copy-start(f32[1,256,256]{2,1,0:T(8,128)} %param.3) | copy-start | bytes 786436
